TPU v7x, 256 devices: a whole 4x4x8 slice. The times are simulated.
256 devices in a mesh: row: 32 (over y, x, core), col: 8 (over z).
Axes of the slice: x: 4, y: 4, z: 8, core: 2. Of those that a mesh axis runs over, the one named last changes fastest.
Arguments:
- gen_points: bfloat16 [16384, 128], P('row'), may hold values from -1.796875 to 1.796875
- ref_points: bfloat16 [65536, 128], P('col'), may hold values from -1.796875 to 1.796875
- gen_mass: float32 [16384], P('row'), may hold values from 0.25 to 4
- ref_mass: float32 [65536], P('col'), may hold values from 0.25 to 4
Outputs:
- sample_side_multiplier: float32 [16384], P('row')
- anchor_side_multiplier: float32 [65536], P('col')
- gen_grad: float32 [16384, 128], P('row')
All inputs are finite; a program needn't handle non-finite values.
Results may differ from a plain program's by a relative error of at most 0.0015.
Values sent between devices are 32-bit elements; how exact they have to be, the bound alone decides.
A program may use at most 64 MiB of HBM per device.

v0:
```python
import math

import jax
import jax.numpy as jnp
from jax import lax
from jax.sharding import PartitionSpec as P

ITERS = 2


smoothing_epsilon = 0.05


def merge_rows(current_largest_exponent, current_partial_sum):
    top = lax.pmax(current_largest_exponent, "col")
    summed = lax.psum(current_partial_sum * jnp.exp(current_largest_exponent - top), "col")
    return (top, summed)


def merge_cols(current_largest_exponent, current_partial_sum):
    top = lax.pmax(current_largest_exponent, "row")
    summed = lax.psum(current_partial_sum * jnp.exp(current_largest_exponent - top), "row")
    return (top, summed)


def local(gen_points, ref_points, gen_mass, ref_mass):
    row_count = gen_points.shape[0]
    col_count = ref_points.shape[0]
    width = gen_points.shape[1]
    all_gen = row_count * lax.axis_size("row")
    gen_sum = lax.psum(jnp.sum(gen_mass), "row")
    ref_sum = lax.psum(jnp.sum(ref_mass), "col")
    logarithmic_left_marginal = jnp.log(gen_mass) - jnp.log(gen_sum)
    logarithmic_right_marginal = jnp.log(ref_mass) - jnp.log(ref_sum)
    gen_wide = gen_points.astype(jnp.float32)
    sq_gen = 0.5 * jnp.sum(gen_wide * gen_wide, axis=1)
    ref_wide = ref_points.astype(jnp.float32)
    sq_ref = 0.5 * jnp.sum(ref_wide * ref_wide, axis=1)
    block_size = math.gcd(col_count, 1024)
    block_count = col_count // block_size
    ref_blocks = ref_points.reshape(block_count, block_size, width)
    sqr_blocks = sq_ref.reshape(block_count, block_size)
    logb_blocks = logarithmic_right_marginal.reshape(block_count, block_size)

    def cost_block_view(embedding_points, squared_norms):
        return (
            sq_gen[:, None]
            + squared_norms[None, :]
            - jnp.dot(gen_points, embedding_points.T, preferred_element_type=jnp.float32)
        )

    def col_partial(sample_side_multiplier):

        def one(items):
            embedding_points, squared_norms = items
            gibbs_exponent = (
                logarithmic_left_marginal[:, None]
                + (
                    sample_side_multiplier[:, None]
                    - cost_block_view(embedding_points, squared_norms)
                )
                / smoothing_epsilon
            )
            current_largest_exponent = jnp.max(gibbs_exponent, axis=0)
            current_partial_sum = jnp.sum(
                jnp.exp(gibbs_exponent - current_largest_exponent[None, :]), axis=0
            )
            return (current_largest_exponent, current_partial_sum)

        current_largest_exponent, current_partial_sum = lax.map(one, (ref_blocks, sqr_blocks))
        return (current_largest_exponent.reshape(col_count), current_partial_sum.reshape(col_count))

    anchor_side_multiplier = jnp.zeros((col_count,), jnp.float32)
    sample_side_multiplier = jnp.zeros((row_count,), jnp.float32)
    for repeat in range(ITERS):
        row_gpot_blocks = anchor_side_multiplier.reshape(block_count, block_size)

        def advance(carry, items):
            embedding_points, squared_norms, logarithmic_gibbs_entries, second_dual_potential = (
                items
            )
            gibbs_exponent = (
                logarithmic_gibbs_entries[None, :]
                + (
                    second_dual_potential[None, :]
                    - cost_block_view(embedding_points, squared_norms)
                )
                / smoothing_epsilon
            )
            newest = jnp.maximum(carry[0], jnp.max(gibbs_exponent, axis=1))
            current_partial_sum = carry[1] * jnp.exp(carry[0] - newest) + jnp.sum(
                jnp.exp(gibbs_exponent - newest[:, None]), axis=1
            )
            return ((newest, current_partial_sum), None)

        row_start = (
            jnp.full((row_count,), -jnp.inf, jnp.float32),
            jnp.zeros((row_count,), jnp.float32),
        )
        result, row_unused = lax.scan(
            advance, row_start, (ref_blocks, sqr_blocks, logb_blocks, row_gpot_blocks)
        )
        current_largest_exponent, current_partial_sum = result
        current_largest_exponent, current_partial_sum = merge_rows(
            current_largest_exponent, current_partial_sum
        )
        sample_side_multiplier = -smoothing_epsilon * (
            current_largest_exponent + jnp.log(current_partial_sum)
        )
        current_largest_exponent, current_partial_sum = col_partial(sample_side_multiplier)
        current_largest_exponent, current_partial_sum = merge_cols(
            current_largest_exponent, current_partial_sum
        )
        anchor_side_multiplier = -smoothing_epsilon * (
            current_largest_exponent + jnp.log(current_partial_sum)
        )
    gpot_blocks = anchor_side_multiplier.reshape(block_count, block_size)

    def accumulate(carry, items):
        embedding_points, squared_norms, logarithmic_gibbs_entries, second_dual_potential = items
        exponent = (
            logarithmic_left_marginal[:, None]
            + logarithmic_gibbs_entries[None, :]
            + (
                sample_side_multiplier[:, None]
                + second_dual_potential[None, :]
                - cost_block_view(embedding_points, squared_norms)
            )
            / smoothing_epsilon
        )
        optimal_plan_matrix = all_gen * jnp.exp(exponent)
        mass_row = carry[0] + jnp.sum(optimal_plan_matrix, axis=1)
        pulled = carry[1] + jnp.dot(
            optimal_plan_matrix.astype(jnp.bfloat16),
            embedding_points,
            preferred_element_type=jnp.float32,
        )
        return ((mass_row, pulled), None)

    start = (jnp.zeros((row_count,), jnp.float32), jnp.zeros((row_count, width), jnp.float32))
    partial_sums, unused = lax.scan(
        accumulate, start, (ref_blocks, sqr_blocks, logb_blocks, gpot_blocks)
    )
    mass_row, pulled = lax.psum((partial_sums[0], partial_sums[1]), "col")
    gen_grad = mass_row[:, None] * gen_wide - pulled
    return (sample_side_multiplier, anchor_side_multiplier, gen_grad)


def solution(mesh):
    return jax.shard_map(
        local,
        mesh=mesh,
        in_specs=(P("row", None), P("col", None), P("row"), P("col")),
        out_specs=(P("row"), P("col"), P("row", None)),
        check_vma=False,
    )
```

profile of v0, /device:TPU:1, one launch (start us, length us, event | category | flops | bytes accessed | tf_op | source)
XLA Modules:
  0.0 819.2 jit_solution(7717166479759271425)
XLA Ops:
  7.3 2.7 multiply_reduce_fusion
  10.8 17.8 %psum.56 = f32[]{:T(128)} all-reduce(f32[]{:T(128)} %reduce_sum.81), channel_id=1, replica_groups=mesh['row'=32,'col'=8] {'col'}, use_global_device_ids=true, to_apply=%region_2.0 | all-reduce | flops 1 | bytes 8 | tf_op jit(solution)/shard_map/psum | solution.py:32
  29.3 15.8 %while.65 = (s32[]{:T(128)}, f32[512]{0:T(512)S(1)}, f32[512]{0:T(512)S(1)}, f32[8,1024]{1,0:T(8,128)S(1)}, f32[512]{0:T(512)S(1)}, /*index=5*/f32[8,1024]{1,0:T...) while((s32[]{:T(128)}, f32[512]{0:T(512)S(1)}, ...), condition=%wide.region_9.10_spmd.clone, body=%wide.region_6.9_spmd.clone.sunk | while | flops 138414592 | bytes 4641396 | solution.py:100
  45.2 10.8 %pmax.28 = f32[512]{0:T(512)S(1)} all-reduce(f32[512]{0:T(512)S(1)} %get-tuple-element.248), channel_id=1, replica_groups=mesh['row'=32,'col'=8] {'col'}, use_global_device_ids=true, to_apply=%region_10.11 | all-reduce | flops 512 | bytes 4096 | tf_op jit(solution)/shard_map/pmax | solution.py:15
  55.9 12.4 %psum.58 = f32[512]{0:T(512)S(1)} all-reduce(f32[512]{0:T(512)S(1)} %exponential_multiply_fusion.1), channel_id=1, replica_groups=mesh['row'=32,'col'=8] {'col'}, use_global_device_ids=true, to_apply=%region_11.12 | all-reduce | flops 512 | bytes 4096 | tf_op jit(solution)/shard_map/psum | solution.py:16
  68.9 74.2 %psum.57 = f32[]{:T(128)} all-reduce(f32[]{:T(128)} %reduce_sum.82), channel_id=1, replica_groups=mesh['row'=32,'col'=8] {'row'}, use_global_device_ids=true, to_apply=%region_4.0 | all-reduce | flops 1 | bytes 8 | tf_op jit(solution)/shard_map/psum | solution.py:31
  143.7 17.3 %while.63 = (s32[]{:T(128)}, f32[8,1024]{1,0:T(8,128)S(1)}, f32[8,1024]{1,0:T(8,128)S(1)}, f32[512]{0:T(512)S(1)}, f32[512]{0:T(512)S(1)}, /*index=5*/f32[512]{0...) while((s32[]{:T(128)}, f32[8,1024]{1,0:T(8,128)S(1)}, ...), condition=%wide.region_15.16_spmd, body=%wide.region_12.15_spmd.sunk | while | flops 138409984 | bytes 4635257 | solution.py:70
  143.8 1.6 fusion.66
  145.9 1.6 fusion.66
  150.3 1.6 fusion.66
  152.4 1.6 fusion.66
  154.6 1.6 fusion.66
  156.8 1.6 fusion.66
  158.9 1.6 fusion.66
  161.1 118.6 %pmax.29 = f32[8192]{0:T(1024)S(1)} all-reduce(f32[8192]{0:T(1024)S(1)} %bitcast.171), channel_id=1, replica_groups=mesh['row'=32,'col'=8] {'row'}, use_global_device_ids=true, to_apply=%region_16.17 | all-reduce | flops 8192 | bytes 65536 | tf_op jit(solution)/shard_map/pmax | solution.py:21
  279.7 123.8 %psum.59 = f32[8192]{0:T(1024)S(1)} all-reduce(f32[8192]{0:T(1024)S(1)} %bitcast_multiply_fusion.1), channel_id=1, replica_groups=mesh['row'=32,'col'=8] {'row'}, use_global_device_ids=true, to_apply=%region_17.18 | all-reduce | flops 8192 | bytes 65536 | tf_op jit(solution)/shard_map/psum | solution.py:22
  403.5 16.4 %while.66 = (s32[]{:T(128)}, f32[512]{0:T(512)S(1)}, f32[512]{0:T(512)S(1)}, f32[8,1024]{1,0:T(8,128)S(1)}, f32[8,1024]{1,0:T(8,128)S(1)}, /*index=5*/f32[512]{0...) while((s32[]{:T(128)}, f32[512]{0:T(512)S(1)}, ...), condition=%wide.region_21.22_spmd.clone, body=%wide.region_18.21_spmd.clone.sunk | while | flops 138414592 | bytes 4653696 | solution.py:100
  403.6 1.6 fusion.73
  405.6 1.6 fusion.73
  407.6 1.6 fusion.73
  409.7 1.6 fusion.73
  411.7 1.6 fusion.73
  413.8 1.6 fusion.73
  415.8 1.6 fusion.73
  417.9 1.6 fusion.73
  419.9 10.7 %pmax.30 = f32[512]{0:T(512)S(1)} all-reduce(f32[512]{0:T(512)S(1)} %get-tuple-element.252), channel_id=1, replica_groups=mesh['row'=32,'col'=8] {'col'}, use_global_device_ids=true, to_apply=%region_22.23 | all-reduce | flops 512 | bytes 4096 | tf_op jit(solution)/shard_map/pmax | solution.py:15
  430.6 12.1 %psum.60 = f32[512]{0:T(512)S(1)} all-reduce(f32[512]{0:T(512)S(1)} %exponential_multiply_fusion), channel_id=1, replica_groups=mesh['row'=32,'col'=8] {'col'}, use_global_device_ids=true, to_apply=%region_23.24 | all-reduce | flops 512 | bytes 4096 | tf_op jit(solution)/shard_map/psum | solution.py:16
  442.7 17.3 %while.64 = (s32[]{:T(128)}, f32[8,1024]{1,0:T(8,128)S(1)}, f32[8,1024]{1,0:T(8,128)S(1)}, f32[512]{0:T(512)S(1)}, f32[512]{0:T(512)S(1)}, /*index=5*/f32[512]{0...) while((s32[]{:T(128)}, f32[8,1024]{1,0:T(8,128)S(1)}, ...), condition=%wide.region_27.28_spmd, body=%wide.region_24.27_spmd.sunk | while | flops 138409984 | bytes 4635257 | solution.py:70
  447.1 1.6 fusion.68
  449.2 1.6 fusion.68
  451.4 1.6 fusion.68
  453.5 1.6 fusion.68
  455.7 1.6 fusion.68
  457.9 1.6 fusion.68
  460.0 131.3 %pmax.31 = f32[8192]{0:T(1024)S(1)} all-reduce(f32[8192]{0:T(1024)S(1)} %bitcast.172), channel_id=1, replica_groups=mesh['row'=32,'col'=8] {'row'}, use_global_device_ids=true, to_apply=%region_28.29 | all-reduce | flops 8192 | bytes 65536 | tf_op jit(solution)/shard_map/pmax | solution.py:21
  591.4 123.8 %psum.61 = f32[8192]{0:T(1024)S(1)} all-reduce(f32[8192]{0:T(1024)S(1)} %bitcast_multiply_fusion), channel_id=1, replica_groups=mesh['row'=32,'col'=8] {'row'}, use_global_device_ids=true, to_apply=%region_29.30 | all-reduce | flops 8192 | bytes 65536 | tf_op jit(solution)/shard_map/psum | solution.py:22
  715.8 27.9 %while.67 = (s32[]{:T(128)}, f32[512]{0:T(512)S(1)}, f32[512,128]{1,0:T(8,128)S(1)}, f32[512]{0:T(512)S(1)}, f32[8,1024]{1,0:T(8,128)S(1)}, /*index=5*/f32[512]{...) while((s32[]{:T(128)}, f32[512]{0:T(512)S(1)}, ...), condition=%wide.region_32.33_spmd.clone, body=%wide.region_30.32_spmd.clone.sunk | while | flops 273809920 | bytes 3329168 | solution.py:141
  715.8 1.9 fusion.78
  719.3 1.9 fusion.78
  722.8 1.9 fusion.78
  726.3 1.9 fusion.78
  729.7 1.9 fusion.78
  733.2 1.9 fusion.78
  736.7 1.9 fusion.78
  740.2 1.9 fusion.78
  744.4 10.7 %psum.62 = f32[512]{0:T(512)S(1)} all-reduce(f32[512]{0:T(512)S(1)} %get-tuple-element.256), channel_id=1, replica_groups=mesh['row'=32,'col'=8] {'col'}, use_global_device_ids=true, to_apply=%region_33.34 | all-reduce | flops 512 | bytes 4096 | tf_op jit(solution)/shard_map/psum | solution.py:144
  755.1 55.5 %all-reduce.2.cloned.1.call-done = f32[512,128]{1,0:T(8,128)} async-done(((f32[512,128]{1,0:T(8,128)}), f32[512,128]{1,0:T(8,128)}) %all-reduce.2.cloned.1.call-update) | async-done | bytes 262160 | tf_op jit(solution)/shard_map/psum | solution.py:144
  810.5 1.8 fusion.39
  (240 shorter events, 47.3 us)
Async XLA Ops:
  7.2 2.9 copy-start.1
  7.2 3.1 copy-start.3
  7.2 803.4 %all-reduce.2.cloned.1.call-start = ((), (), s32[]{:S(2)}) async-start(), calls=%async_computation | async-start | bytes 524288 | tf_op jit(solution)/shard_map/psum | solution.py:144
  29.3 39.0 %copy-start.4 = (f32[512]{0:T(512)S(1)}, f32[512]{0:T(512)}, u32[]{:S(2)}) copy-start(f32[512]{0:T(512)} %param.16) | copy-start | bytes 6148
  715.2 0.6 copy-start.2
  743.6 0.7 copy-start
  743.7 68.7 %copy-start.5 = (f32[512]{0:T(512)}, f32[512]{0:T(512)S(1)}, u32[]{:S(2)}) copy-start(f32[512]{0:T(512)S(1)} %get-tuple-element.962) | copy-start | bytes 6148
Sparse Core Ops, SparseCore 0:
  744.5 65.9 all-reduce.1
where the time goes:
time: 825 us; the launch traced here: 819 us
  blocking collectives  646 us (78%)
  matrix products  77.2 us (9%)
  waiting for transfers between devices  55.5 us (7%)
  other arithmetic  17.7 us (2%)
  between operations  15.5 us (2%)
    pmax x2, blocking collectives, merge_cols(): top = lax.pmax(current_largest_exponent, 'row')  250 us
    psum x2, blocking collectives, merge_cols(): lax.psum(current_partial_sum * jnp.exp(current_largest_exponent - top), '...  248 us
    psum x1, blocking collectives, local(): gen_sum = lax.psum(jnp.sum(gen_mass), 'row')  74.2 us
    dot_general x40, matrix products, cost_block_view(): jnp.dot(gen_points, embedding_points.T, preferred_element_type=jnp.float32)  65.6 us
    psum x1, waiting for transfers between devices, local(): mass_row, pulled = lax.psum((partial_sums[0], partial_sums[1]), 'col')  55.5 us
    psum x2, blocking collectives, merge_rows(): lax.psum(current_partial_sum * jnp.exp(current_largest_exponent - top), '...  24.5 us
    pmax x2, blocking collectives, merge_rows(): top = lax.pmax(current_largest_exponent, 'col')  21.4 us
    psum x1, blocking collectives, local(): ref_sum = lax.psum(jnp.sum(ref_mass), 'col')  17.8 us
  transfers between devices with their start and end apart: 1, of which 1 were waited for; matrix products, arithmetic and copies ran while one was open for 0% of the time, Pallas kernels for 0%

commit v1 on v0

v1 whole, which is shorter than its diff:
```python
import math

import jax
import jax.numpy as jnp
from jax import lax
from jax.experimental import pallas as pl
from jax.experimental.pallas import tpu as pltpu
from jax.sharding import PartitionSpec as P

smoothing_epsilon = 0.05
SCALE = 1.0 / (smoothing_epsilon * math.log(2.0))
LANES = 128
SUB = 8
LOWEST = -3.0e38
f32 = jnp.float32
MESH = pl.DeviceIdType.MESH

CHUNK = 64
TILE1 = 1024
TILE2 = 1024
GROUPS3 = 16
GROUPS4 = 4
TILE5 = 2048
ROWS5 = 128


def scores(a, b):
    return lax.dot_general(a, b, (((1,), (1,)), ((), ())), preferred_element_type=f32)


def lane_cols(group):
    return pl.ds(pl.multiple_of(group * LANES, LANES), LANES)


def total(v):
    return jnp.sum(jnp.sum(v, axis=0, keepdims=True), axis=1, keepdims=True)


def kernel(
    nrow, ncol, x, y, gm, rm, f_out, g_out, grad_out,
    R, MH, beta, acc_a, acc_b, lanes_u,
    zs1, zr1, cs2, cr2, gs2, gr2, zs3, zr3, cs4, cr4, gs4, gr4, pull, part, pr5, done,
    send_sem, recv_sem,
):
    rows, width = x.shape
    cols = y.shape[0]
    row_blocks = rows // LANES
    groups = cols // LANES
    per = groups // nrow
    r = lax.axis_index("row")
    c = lax.axis_index("col")

    def row_peer(s):
        return lax.rem(r + s, nrow)

    def col_peer(s):
        return lax.rem(c + s, ncol)

    barrier = pltpu.get_barrier_semaphore()

    def greet_row(s, carry):
        pl.semaphore_signal(barrier, inc=1, device_id={"row": row_peer(s)}, device_id_type=MESH)
        return carry

    def greet_col(s, carry):
        pl.semaphore_signal(barrier, inc=1, device_id={"col": col_peer(s)}, device_id_type=MESH)
        return carry

    lax.fori_loop(1, nrow, greet_row, 0)
    lax.fori_loop(1, ncol, greet_col, 0)

    def exchange(phase, count, peer, axis, source, target):
        def one(s, carry):
            k = peer(s)
            pltpu.make_async_remote_copy(
                src_ref=source(k),
                dst_ref=target,
                send_sem=send_sem.at[phase],
                recv_sem=recv_sem.at[phase],
                device_id={axis: k},
                device_id_type=MESH,
            ).start()
            return carry

        lax.fori_loop(1, count, one, 0)

    def arrived(phase, whole):
        pltpu.make_async_copy(whole, whole, recv_sem.at[phase]).wait()

    def left(phase, whole):
        pltpu.make_async_copy(whole, whole, send_sem.at[phase]).wait()

    def norms(b, carry):
        wide = y[pl.ds(pl.multiple_of(b * 1024, 1024), 1024), :].astype(f32)
        squares = wide * wide
        for k in range(8):
            half = jnp.sum(squares[k * LANES:(k + 1) * LANES].T, axis=0, keepdims=True)
            beta[pl.ds(b * 8 + k, 1), :] = half
        return carry

    lax.fori_loop(0, cols // 1024, norms, 0)
    log_ref = jnp.log2(rm[...])
    beta[...] = log_ref - (0.5 * SCALE) * beta[...]

    acc_a[...] = jnp.full(acc_a.shape, LOWEST, f32)
    acc_b[...] = jnp.zeros(acc_b.shape, f32)
    n1 = TILE1 // LANES

    def pass1(t, carry):
        block = scores(x[...], y[pl.ds(pl.multiple_of(t * TILE1, TILE1), TILE1), :])
        bias = [beta[pl.ds(t * n1 + k, 1), :] for k in range(n1)]
        for i in range(0, rows, SUB):
            e = [block[i:i + SUB, k * LANES:(k + 1) * LANES] * SCALE + bias[k] for k in range(n1)]
            old = acc_a[i:i + SUB, :]
            top = e[0]
            for v in e[1:]:
                top = jnp.maximum(top, v)
            top = jnp.maximum(top, old)
            s = acc_b[i:i + SUB, :] * jnp.exp2(old - top)
            for v in e:
                s = s + jnp.exp2(v - top)
            acc_a[i:i + SUB, :] = top
            acc_b[i:i + SUB, :] = s
        return carry

    lax.fori_loop(0, cols // TILE1, pass1, 0)

    for k in range(row_blocks):
        part_rows = slice(k * LANES, (k + 1) * LANES)
        v = (acc_a[part_rows, :] + jnp.log2(acc_b[part_rows, :])).T
        top = jnp.max(v, axis=0, keepdims=True)
        zs1[k:k + 1, :] = top + jnp.log2(jnp.sum(jnp.exp2(v - top), axis=0, keepdims=True))
    zs1[row_blocks:, :] = jnp.broadcast_to(total(rm[...]), (SUB - row_blocks, LANES))

    pl.semaphore_wait(barrier, (nrow - 1) + (ncol - 1))

    exchange(0, ncol, col_peer, "col", lambda k: zs1, zr1.at[c])
    zr1[c] = zs1[...]
    arrived(0, zr1.at[pl.ds(0, ncol - 1)])
    v = zr1[...]
    top = jnp.max(v, axis=0)
    lse = top + jnp.log2(jnp.sum(jnp.exp2(v - top[None]), axis=0))
    ref_total = jnp.sum(v, axis=0)[row_blocks:row_blocks + 1, :]
    row_lse = lse[:row_blocks, :] - jnp.log2(ref_total)
    alpha = jnp.log2(gm[...]) - row_lse
    for k in range(row_blocks):
        lanes_u[k * LANES:(k + 1) * LANES, :] = jnp.broadcast_to(alpha[k:k + 1, :], (LANES, LANES)).T

    n2 = TILE2 // LANES
    cs2[:, per:, :] = jnp.broadcast_to(total(gm[...])[None], (nrow, cs2.shape[1] - per, LANES))

    def pass2(t, carry):
        block = scores(x[...], y[pl.ds(pl.multiple_of(t * TILE2, TILE2), TILE2), :])
        bias = [beta[pl.ds(t * n2 + k, 1), :] for k in range(n2)]
        tops = [jnp.full((SUB, LANES), LOWEST, f32) for _ in range(n2)]
        sums = [jnp.zeros((SUB, LANES), f32) for _ in range(n2)]
        for q in range(rows // CHUNK):
            span = range(q * CHUNK, (q + 1) * CHUNK, SUB)
            al = [lanes_u[i:i + SUB, :] for i in span]
            for k in range(n2):
                e = [block[i:i + SUB, k * LANES:(k + 1) * LANES] * SCALE + a for i, a in zip(span, al)]
                top = tops[k]
                for v in e:
                    top = jnp.maximum(top, v)
                s = sums[k] * jnp.exp2(tops[k] - top)
                for i, v in zip(span, e):
                    z = jnp.exp2(v - top)
                    R[i:i + SUB, lane_cols(t * n2 + k)] = z
                    s = s + z
                tops[k] = top
                sums[k] = s
                MH[q * SUB:(q + 1) * SUB, lane_cols(t * n2 + k)] = top + bias[k]
        for k in range(n2):
            top = jnp.max(tops[k], axis=0, keepdims=True)
            s = jnp.sum(sums[k] * jnp.exp2(tops[k] - top), axis=0, keepdims=True)
            cs2[t * (n2 // per) + k // per, k % per:k % per + 1, :] = top + jnp.log2(s) + bias[k]
        return carry

    lax.fori_loop(0, cols // TILE2, pass2, 0)

    exchange(1, nrow, row_peer, "row", lambda k: cs2.at[k], cr2.at[r])
    cr2[r] = cs2[r]
    arrived(1, cr2.at[pl.ds(0, nrow - 1)])
    v = cr2[...]
    top = jnp.max(v, axis=0)
    lse = top + jnp.log2(jnp.sum(jnp.exp2(v - top[None]), axis=0))
    gs2[:per, :] = lse[:per, :]
    gen_total = jnp.sum(v, axis=0)[per:per + 1, :]
    exchange(2, nrow, row_peer, "row", lambda k: gs2, gr2.at[r])
    gr2[r] = gs2[...]
    arrived(2, gr2.at[pl.ds(0, nrow - 1)])

    def weigh(b, carry):
        for h in range(per):
            g = b * per + h
            ref_share = rm[pl.ds(g, 1), :] / ref_total
            col = gr2[b, h:h + 1, :]
            v = MH[:, lane_cols(g)]
            MH[:, lane_cols(g)] = jnp.exp2(v - col) * ref_share
        return carry

    lax.fori_loop(0, nrow, weigh, 0, unroll=4)

    acc_a[...] = jnp.zeros(acc_a.shape, f32)

    def pass3(t, carry):
        for q in range(rows // CHUNK):
            w = [MH[q * SUB:(q + 1) * SUB, lane_cols(t * GROUPS3 + k)] for k in range(GROUPS3)]
            for i in range(q * CHUNK, (q + 1) * CHUNK, SUB):
                even = acc_a[i:i + SUB, :]
                odd = jnp.zeros((SUB, LANES), f32)
                for k in range(GROUPS3):
                    v = R[i:i + SUB, lane_cols(t * GROUPS3 + k)] * w[k]
                    if k % 2:
                        odd = odd + v
                    else:
                        even = even + v
                acc_a[i:i + SUB, :] = even + odd
        return carry

    lax.fori_loop(0, groups // GROUPS3, pass3, 0)
    for k in range(row_blocks):
        zs3[k:k + 1, :] = jnp.sum(acc_a[k * LANES:(k + 1) * LANES, :].T, axis=0, keepdims=True)
    exchange(3, ncol, col_peer, "col", lambda k: zs3, zr3.at[c])
    zr3[c] = zs3[...]
    arrived(3, zr3.at[pl.ds(0, ncol - 1)])
    u = gm[...] / (gen_total * jnp.sum(zr3[...], axis=0))
    for k in range(row_blocks):
        lanes_u[k * LANES:(k + 1) * LANES, :] = jnp.broadcast_to(u[k:k + 1, :], (LANES, LANES)).T
        wide = x[k * LANES:(k + 1) * LANES, :].astype(f32)
        half = 0.5 * jnp.sum((wide * wide).T, axis=0, keepdims=True)
        f_out[k:k + 1, :] = half + (jnp.log2(u[k:k + 1, :]) - row_lse[k:k + 1, :]) * (1.0 / SCALE)

    def pass4(t, carry):
        sums = [jnp.zeros((SUB, LANES), f32) for _ in range(GROUPS4)]
        for q in range(rows // CHUNK):
            inner = [jnp.zeros((SUB, LANES), f32) for _ in range(GROUPS4)]
            for i in range(q * CHUNK, (q + 1) * CHUNK, SUB):
                a = lanes_u[i:i + SUB, :]
                for k in range(GROUPS4):
                    inner[k] = inner[k] + R[i:i + SUB, lane_cols(t * GROUPS4 + k)] * a
            for k in range(GROUPS4):
                sums[k] = sums[k] + inner[k] * MH[q * SUB:(q + 1) * SUB, lane_cols(t * GROUPS4 + k)]
        for k in range(GROUPS4):
            cs4[t * (GROUPS4 // per) + k // per, k % per:k % per + 1, :] = jnp.sum(sums[k], axis=0, keepdims=True)
        return carry

    lax.fori_loop(0, groups // GROUPS4, pass4, 0)

    exchange(4, nrow, row_peer, "row", lambda k: cs4.at[k], cr4.at[r])
    cr4[r] = cs4[r]
    arrived(4, cr4.at[pl.ds(0, nrow - 1)])
    plan_cols = jnp.sum(cr4[...], axis=0)
    for h in range(per):
        gs4[h:h + 1, :] = rm[pl.ds(r * per + h, 1), :] / (ref_total * plan_cols[h:h + 1, :])
    exchange(5, nrow, row_peer, "row", lambda k: gs4, gr4.at[r])
    gr4[r] = gs4[...]
    arrived(5, gr4.at[pl.ds(0, nrow - 1)])

    acc_a[...] = jnp.zeros(acc_a.shape, f32)
    pull[...] = jnp.zeros(pull.shape, f32)
    lanes_u[...] = lanes_u[...] * float(rows * nrow)
    n5 = TILE5 // LANES

    def pass5(t, carry):
        points = y[pl.ds(pl.multiple_of(t * TILE5, TILE5), TILE5), :]
        ratio = [gr4[t * (n5 // per) + k // per, k % per:k % per + 1, :] for k in range(n5)]
        for i0 in range(0, rows, ROWS5):
            low = [[] for _ in range(n5)]
            for q in range(i0 // CHUNK, (i0 + ROWS5) // CHUNK):
                w = [MH[q * SUB:(q + 1) * SUB, lane_cols(t * n5 + k)] * ratio[k] for k in range(n5)]
                for i in range(q * CHUNK, (q + 1) * CHUNK, SUB):
                    a = lanes_u[i:i + SUB, :]
                    mass = acc_a[i:i + SUB, :]
                    for k in range(n5):
                        p = (R[i:i + SUB, lane_cols(t * n5 + k)] * w[k]) * a
                        mass = mass + p
                        low[k].append(p)
                    acc_a[i:i + SUB, :] = mass
            plan_low = jnp.concatenate(
                [jnp.concatenate(v, axis=0).astype(jnp.bfloat16) for v in low], axis=1
            )
            pull[i0:i0 + ROWS5, :] += jnp.dot(plan_low, points, preferred_element_type=f32)
        return carry

    lax.fori_loop(0, cols // TILE5, pass5, 0)

    mass_row = jnp.sum(acc_a[...], axis=1, keepdims=True)
    part[...] = mass_row * x[...].astype(f32) - pull[...]

    share = rows // ncol

    def rows_of(k):
        return pl.ds(pl.multiple_of(k * share, share), share)

    exchange(6, ncol, col_peer, "col", lambda k: part.at[rows_of(k)], pr5.at[c])
    pr5[c] = part[rows_of(c), :]

    log_total = jnp.log2(gen_total)
    for b in range(nrow):
        for h in range(per):
            g = b * per + h
            g_out[g:g + 1, :] = (
                (log_total + jnp.log2(rm[g:g + 1, :]) - gr2[b, h:h + 1, :])
                + jnp.log2(gr4[b, h:h + 1, :])
            ) * (1.0 / SCALE)

    arrived(6, pr5.at[pl.ds(0, ncol - 1)])
    done[rows_of(c), :] = jnp.sum(pr5[...], axis=0)
    exchange(7, ncol, col_peer, "col", lambda k: done.at[rows_of(c)], done.at[rows_of(c)])
    arrived(7, done.at[pl.ds(0, rows - share)])
    grad_out[...] = done[...]

    left(0, zr1.at[pl.ds(0, ncol - 1)])
    left(1, cr2.at[pl.ds(0, nrow - 1)])
    left(2, gr2.at[pl.ds(0, nrow - 1)])
    left(3, zr3.at[pl.ds(0, ncol - 1)])
    left(4, cr4.at[pl.ds(0, nrow - 1)])
    left(5, gr4.at[pl.ds(0, nrow - 1)])
    left(6, pr5.at[pl.ds(0, ncol - 1)])
    left(7, done.at[pl.ds(0, rows - share)])


def local(nrow, ncol, gen_points, ref_points, gen_mass, ref_mass):
    rows, width = gen_points.shape
    cols = ref_points.shape[0]
    row_blocks = rows // LANES
    groups = cols // LANES
    per = groups // nrow
    chunks = rows // CHUNK
    vmem = pl.BlockSpec(memory_space=pltpu.VMEM)

    def buf(*shape):
        return pltpu.VMEM(shape, f32)

    def body(*refs):
        kernel(nrow, ncol, *refs)

    f, g, grad = pl.pallas_call(
        body,
        out_shape=(
            jax.ShapeDtypeStruct((row_blocks, LANES), f32),
            jax.ShapeDtypeStruct((groups, LANES), f32),
            jax.ShapeDtypeStruct((rows, width), f32),
        ),
        in_specs=[vmem] * 4,
        out_specs=(vmem, vmem, vmem),
        scratch_shapes=[
            buf(rows, cols), buf(chunks * SUB, cols), buf(groups, LANES),
            buf(rows, LANES), buf(rows, LANES), buf(rows, LANES),
            buf(SUB, LANES), buf(ncol, SUB, LANES),
            buf(nrow, 2 * per, LANES), buf(nrow, 2 * per, LANES),
            buf(per, LANES), buf(nrow, per, LANES),
            buf(row_blocks, LANES), buf(ncol, row_blocks, LANES),
            buf(nrow, per, LANES), buf(nrow, per, LANES),
            buf(per, LANES), buf(nrow, per, LANES),
            buf(rows, width), buf(rows, width), buf(ncol, rows // ncol, width), buf(rows, width),
            pltpu.SemaphoreType.DMA((8,)),
            pltpu.SemaphoreType.DMA((8,)),
        ],
        compiler_params=pltpu.CompilerParams(
            collective_id=0, has_side_effects=True, vmem_limit_bytes=56 * 2**20
        ),
        name="sinkhorn",
    )(gen_points, ref_points, gen_mass.reshape(row_blocks, LANES), ref_mass.reshape(groups, LANES))
    return f.reshape(rows), g.reshape(cols), grad


def solution(mesh):
    nrow, ncol = mesh.shape["row"], mesh.shape["col"]

    def run(*args):
        return local(nrow, ncol, *args)

    return jax.shard_map(
        run,
        mesh=mesh,
        in_specs=(P("row", None), P("col", None), P("row"), P("col")),
        out_specs=(P("row"), P("col"), P("row", None)),
        check_vma=False,
    )
```

time: 825 us -> 82.6 us (0.10)
  blocking collectives: 646 us -> 0 us
  Pallas kernels: 0 us -> 77.4 us
  matrix products: 77.2 us -> 0 us
  waiting for transfers between devices: 55.5 us -> 0 us
  other arithmetic: 17.7 us -> 0 us
  between operations: 15.5 us -> 0.64 us
    psum x7 -> x0, blocking collectives: 375 us -> none  [the longest x2 248 us: merge_cols(): lax.psum(current_partial_sum * jnp.exp(current_largest_exponent - top), '...]
    pmax x4 -> x0, blocking collectives: 271 us -> none  [the longest x2 250 us: merge_cols(): top = lax.pmax(current_largest_exponent, 'row')]
    pallas_call x0 -> x1, Pallas kernels: none -> 77.4 us  [local(): pl.pallas_call(body, out_shape=(jax.ShapeDtypeStruct((row_blocks, LANES),...]
    dot_general x48 -> x0, matrix products: 77.2 us -> none  [the longest x40 65.6 us: cost_block_view(): jnp.dot(gen_points, embedding_points.T, preferred_element_type=jnp.float32)]
    psum x1 -> x0, waiting for transfers between devices: 55.5 us -> none  [local(): mass_row, pulled = lax.psum((partial_sums[0], partial_sums[1]), 'col')]
    reduce_sum x36 -> x0, other arithmetic: 15.3 us -> none  [the longest x16 5.79 us: advance(): jnp.sum(jnp.exp(gibbs_exponent - newest[:, None]), axis=1)]
  transfers between devices with their start and end apart: 1 -> 0, of which waited for: 1 -> 0; matrix products, arithmetic and copies ran while one was open for 0% -> 0% of each run, Pallas kernels for 0% -> 0%
where the time goes in v1:
time: 82.6 us; the launch traced here: 82.4 us
  Pallas kernels  77.4 us (94%)
  local copies, waits for them, and re-layouts  4.3 us (5%)
    pallas_call x1, Pallas kernels, local(): pl.pallas_call(body, out_shape=(jax.ShapeDtypeStruct((row_blocks, LANES),...  77.4 us
    unnamed x3, local copies, waits for them, and re-layouts  4.3 us

profile of v1, /device:TPU:1, one launch (start us, length us, event | category | flops | bytes accessed | tf_op | source)
XLA Modules:
  0.0 82.4 jit_solution(1752906795952599361)
XLA Ops:
  0.6 77.4 %sinkhorn.1 = (f32[4,128]{1,0:T(4,128)}, f32[64,128]{1,0:T(8,128)}, f32[512,128]{1,0:T(8,128)}) custom-call(bf16[512,128]{1,0:T(8,128)(2,1)} %refs_0_.1, bf16[8192,128]{1,0:T(8,128)(2,1)} %refs_1_.1, f32[4,128]{1,0:T(4,128)} %bitcast.6, f32[64,128]{1,0:T(8,128)} %bitcast.4), custom_call_target="tpu_custom_call" | custom-call | tf_op jit(solution)/shard_map/sinkhorn/pallas_call | solution.py:339
  78.1 1.3 %copy.10 = f32[512]{0:T(512)} copy(f32[512]{0:T(512)} %bitcast.7) | data formatting | bytes 4096
  79.3 1.4 %copy.11 = f32[8192]{0:T(1024)} copy(f32[8192]{0:T(1024)} %bitcast.5) | data formatting | bytes 65536
  80.7 1.7 %copy.12 = f32[512,128]{1,0:T(8,128)} copy(f32[512,128]{1,0:T(8,128)} %get-tuple-element.14) | data formatting | bytes 524288

commit v2 on v1

v2 whole, which is shorter than its diff:
```python
import math

import jax
import jax.numpy as jnp
from jax import lax
from jax.experimental import pallas as pl
from jax.experimental.pallas import tpu as pltpu
from jax.sharding import PartitionSpec as P

smoothing_epsilon = 0.05
SCALE = 1.0 / (smoothing_epsilon * math.log(2.0))
LANES = 128
SUB = 8
LOWEST = -3.0e38
f32 = jnp.float32
MESH = pl.DeviceIdType.MESH

CHUNK = 64
TILE1 = 2048
TILE2 = 2048
GROUPS3 = 16
GROUPS4 = 4
TILE5 = 2048
ROWS5 = 128
PARTS = 2


def scores(a, b):
    return lax.dot_general(a, b, (((1,), (1,)), ((), ())), preferred_element_type=f32)


def lane_cols(group):
    return pl.ds(pl.multiple_of(group * LANES, LANES), LANES)


def tile_rows(t):
    return pl.ds(pl.multiple_of(t * SUB, SUB), SUB)


def total(v):
    return jnp.sum(jnp.sum(v, axis=0, keepdims=True), axis=1, keepdims=True)


def log_sum(v):
    top = jnp.max(v, axis=0)
    return top + jnp.log2(jnp.sum(jnp.exp2(v - top[None]), axis=0))


def kernel(
    nrow, ncol, x, y, gm, rm, f_out, g_out, grad_out,
    R, MH, TOP, SUM, beta, acc_a, acc_b, lanes_u, row_f,
    sa, ra, ca, ta, zs1, zr1, zs3, zr3,
    cs2, cr2, gs2, ag2, col2, cs4, cr4, gs4, ag4, col4,
    pull, part, pr5, done, send_sem, recv_sem,
):
    rows, width = x.shape
    cols = y.shape[0]
    row_blocks = rows // LANES
    groups = cols // LANES
    tiles = groups // SUB
    half_tiles = tiles // 2
    half_groups = groups // 2
    chips = nrow // 2
    part_rows = rows // PARTS
    part_blocks = part_rows // LANES
    r = lax.axis_index("row")
    c = lax.axis_index("col")
    core = lax.rem(r, 2)
    chip = r // 2
    partner = 2 * chip + (1 - core)
    own = core * half_tiles
    other = (1 - core) * half_tiles

    def chip_peer(s):
        return lax.rem(r + 2 * s, nrow)

    def col_peer(s):
        return lax.rem(c + s, ncol)

    barrier = pltpu.get_barrier_semaphore()

    def greet_row(s, carry):
        pl.semaphore_signal(barrier, inc=1, device_id={"row": chip_peer(s)}, device_id_type=MESH)
        return carry

    def greet_col(s, carry):
        pl.semaphore_signal(barrier, inc=1, device_id={"col": col_peer(s)}, device_id_type=MESH)
        return carry

    pl.semaphore_signal(barrier, inc=1, device_id={"row": partner}, device_id_type=MESH)
    lax.fori_loop(1, chips, greet_row, 0)
    lax.fori_loop(1, ncol, greet_col, 0)

    def send(phase, device, source, target):
        pltpu.make_async_remote_copy(
            src_ref=source,
            dst_ref=target,
            send_sem=send_sem.at[phase],
            recv_sem=recv_sem.at[phase],
            device_id=device,
            device_id_type=MESH,
        ).start()

    def to_chips(phase, source, target):
        def one(s, carry):
            send(phase, {"row": chip_peer(s)}, source, target)
            return carry

        lax.fori_loop(1, chips, one, 0)

    def to_cols(phase, source, target):
        def one(s, carry):
            k = col_peer(s)
            send(phase, {"col": k}, source(k), target)
            return carry

        lax.fori_loop(1, ncol, one, 0)

    def arrived(phase, whole):
        pltpu.make_async_copy(whole, whole, recv_sem.at[phase]).wait()

    def left(phase, whole):
        pltpu.make_async_copy(whole, whole, send_sem.at[phase]).wait()

    Z1, Z3, CORE2, CHIP2, BACK2, CORE4, CHIP4, BACK4, RS, AG, A1, A2 = (
        0, 2, 4, 8, 12, 13, 17, 21, 22, 26, 30, 31,
    )

    def norms(b, carry):
        wide = y[pl.ds(pl.multiple_of(b * 1024, 1024), 1024), :].astype(f32)
        squares = wide * wide
        for k in range(8):
            half = jnp.sum(squares[k * LANES:(k + 1) * LANES].T, axis=0, keepdims=True)
            beta[pl.ds(b * 8 + k, 1), :] = half
        return carry

    lax.fori_loop(0, cols // 1024, norms, 0)
    log_ref = jnp.log2(rm[...])
    beta[...] = log_ref - (0.5 * SCALE) * beta[...]
    zs1[...] = jnp.broadcast_to(total(rm[...])[None], zs1.shape)
    sa[...] = jnp.broadcast_to(total(gm[...]), sa.shape)

    acc_a[...] = jnp.full(acc_a.shape, LOWEST, f32)
    acc_b[...] = jnp.zeros(acc_b.shape, f32)
    n1 = TILE1 // LANES

    def pass1(h, t):
        block = scores(x[h * part_rows:(h + 1) * part_rows, :], y[pl.ds(pl.multiple_of(t * TILE1, TILE1), TILE1), :])
        bias = [beta[pl.ds(t * n1 + k, 1), :] for k in range(n1)]
        for i in range(0, part_rows, SUB):
            o = h * part_rows + i
            e = [block[i:i + SUB, k * LANES:(k + 1) * LANES] * SCALE + bias[k] for k in range(n1)]
            old = acc_a[o:o + SUB, :]
            top = e[0]
            for v in e[1:]:
                top = jnp.maximum(top, v)
            top = jnp.maximum(top, old)
            s = acc_b[o:o + SUB, :] * jnp.exp2(old - top)
            for v in e:
                s = s + jnp.exp2(v - top)
            acc_a[o:o + SUB, :] = top
            acc_b[o:o + SUB, :] = s

    for h in range(PARTS):
        def pass1_tile(t, carry, h=h):
            pass1(h, t)
            return carry

        lax.fori_loop(0, cols // TILE1, pass1_tile, 0)
        for k in range(part_blocks):
            o = (h * part_blocks + k) * LANES
            v = (acc_a[o:o + LANES, :] + jnp.log2(acc_b[o:o + LANES, :])).T
            top = jnp.max(v, axis=0, keepdims=True)
            zs1[h, k:k + 1, :] = top + jnp.log2(jnp.sum(jnp.exp2(v - top), axis=0, keepdims=True))
        if h == 0:
            pl.semaphore_wait(barrier, chips + ncol - 1)
            send(A1, {"row": partner}, sa, ra)
        to_cols(Z1 + h, lambda k: zs1.at[h], zr1.at[h, c])
        zr1[h, c] = zs1[h]

    n2 = TILE2 // LANES
    t2 = n2 // SUB

    def row_weights(v, h):
        for k in range(part_blocks):
            o = (h * part_blocks + k) * LANES
            lanes_u[o:o + LANES, :] = jnp.broadcast_to(v[k:k + 1, :], (LANES, LANES)).T

    def pass2(h, g0):
        block = scores(
            x[h * part_rows:(h + 1) * part_rows, :],
            y[pl.ds(pl.multiple_of(g0 * LANES, TILE2), TILE2), :],
        )
        bias = [beta[pl.ds(g0 + k, 1), :] for k in range(n2)]
        tops = [TOP[:, lane_cols(g0 + k)] if h else jnp.full((SUB, LANES), LOWEST, f32) for k in range(n2)]
        sums = [SUM[:, lane_cols(g0 + k)] if h else jnp.zeros((SUB, LANES), f32) for k in range(n2)]
        for q in range(part_rows // CHUNK):
            span = range(q * CHUNK, (q + 1) * CHUNK, SUB)
            o = h * part_rows
            al = [lanes_u[o + i:o + i + SUB, :] for i in span]
            hq = (h * (part_rows // CHUNK) + q) * SUB
            for k in range(n2):
                e = [block[i:i + SUB, k * LANES:(k + 1) * LANES] * SCALE + a for i, a in zip(span, al)]
                top = tops[k]
                for v in e:
                    top = jnp.maximum(top, v)
                s = sums[k] * jnp.exp2(tops[k] - top)
                for i, v in zip(span, e):
                    z = jnp.exp2(v - top)
                    R[o + i:o + i + SUB, lane_cols(g0 + k)] = z
                    s = s + z
                tops[k] = top
                sums[k] = s
                MH[hq:hq + SUB, lane_cols(g0 + k)] = top + bias[k]
        if h < PARTS - 1:
            for k in range(n2):
                TOP[:, lane_cols(g0 + k)] = tops[k]
                SUM[:, lane_cols(g0 + k)] = sums[k]
            return
        for k in range(n2):
            top = jnp.max(tops[k], axis=0, keepdims=True)
            s = jnp.sum(sums[k] * jnp.exp2(tops[k] - top), axis=0, keepdims=True)
            cs2[pl.ds(g0 + k, 1), :] = top + jnp.log2(s) + bias[k]

    def log_of_rows(h):
        arrived(Z1 + h, zr1.at[h, pl.ds(0, ncol - 1)])
        v = zr1[h]
        lse = log_sum(v)[:part_blocks, :]
        ref_total = jnp.sum(v, axis=0)[part_blocks:part_blocks + 1, :]
        row_lse = lse - jnp.log2(ref_total)
        block = slice(h * part_blocks, (h + 1) * part_blocks)
        row_f[block, :] = row_lse
        row_weights(jnp.log2(gm[block, :]) - row_lse, h)
        return ref_total

    for h in range(PARTS - 1):
        ref_total = log_of_rows(h)

        def pass2_tile(t, carry, h=h):
            pass2(h, t * n2)
            return carry

        lax.fori_loop(0, groups // n2, pass2_tile, 0)
    arrived(A1, ra)
    ca[...] = sa[...] + ra[...]
    to_chips(A2, ca, ta.at[chip])
    ta[chip] = ca[...]
    log_of_rows(PARTS - 1)

    def pass2_other(t, carry):
        g0 = other * SUB + t * n2
        pass2(PARTS - 1, g0)
        for j in range(t2):
            at = tile_rows(other + t * t2 + j)
            send(CORE2 + t * t2 + j, {"row": partner}, cs2.at[at], cr2.at[at])
        return carry

    def pass2_own(t, carry):
        g0 = own * SUB + t * n2
        pass2(PARTS - 1, g0)
        for j in range(t2):
            at = tile_rows(own + t * t2 + j)
            mine = tile_rows(t * t2 + j)
            arrived(CORE2 + t * t2 + j, cr2.at[at])
            a, b = cs2[at, :], cr2[at, :]
            top = jnp.maximum(a, b)
            both = top + jnp.log2(jnp.exp2(a - top) + jnp.exp2(b - top))
            gs2[mine, :] = both
            ag2[chip, mine, :] = both
            to_chips(CHIP2 + t * t2 + j, gs2.at[mine], ag2.at[chip, mine])
        return carry

    lax.fori_loop(0, half_groups // n2, pass2_other, 0)
    lax.fori_loop(0, half_groups // n2, pass2_own, 0)

    for j in range(half_tiles):
        mine = slice(j * SUB, (j + 1) * SUB)
        arrived(CHIP2 + j, ag2.at[pl.ds(0, chips - 1), mine])
        col2[tile_rows(own + j), :] = log_sum(ag2[:, mine, :])
    own_groups = pl.ds(pl.multiple_of(own * SUB, SUB), half_groups)
    other_groups = pl.ds(pl.multiple_of(other * SUB, SUB), half_groups)
    send(BACK2, {"row": partner}, col2.at[own_groups], col2.at[own_groups])

    def weigh(first):
        def one(j, carry):
            g = first * SUB + j
            ref_share = rm[pl.ds(g, 1), :] / ref_total
            MH[:, lane_cols(g)] = jnp.exp2(MH[:, lane_cols(g)] - col2[pl.ds(g, 1), :]) * ref_share
            return carry

        lax.fori_loop(0, half_groups, one, 0, unroll=4)

    def pass3(first, h):
        def tile(t, carry):
            g0 = first * SUB + t * GROUPS3
            for q in range(part_rows // CHUNK):
                hq = (h * (part_rows // CHUNK) + q) * SUB
                w = [MH[hq:hq + SUB, lane_cols(g0 + k)] for k in range(GROUPS3)]
                for i in range(h * part_rows + q * CHUNK, h * part_rows + (q + 1) * CHUNK, SUB):
                    even = acc_a[i:i + SUB, :]
                    odd = jnp.zeros((SUB, LANES), f32)
                    for k in range(GROUPS3):
                        v = R[i:i + SUB, lane_cols(g0 + k)] * w[k]
                        if k % 2:
                            odd = odd + v
                        else:
                            even = even + v
                    acc_a[i:i + SUB, :] = even + odd
            return carry

        lax.fori_loop(0, half_groups // GROUPS3, tile, 0)

    acc_a[...] = jnp.zeros(acc_a.shape, f32)
    weigh(own)
    for h in range(PARTS):
        pass3(own, h)
    arrived(BACK2, col2.at[other_groups])
    weigh(other)
    for h in range(PARTS):
        pass3(other, h)
        for k in range(part_blocks):
            o = (h * part_blocks + k) * LANES
            zs3[h, k:k + 1, :] = jnp.sum(acc_a[o:o + LANES, :].T, axis=0, keepdims=True)
        to_cols(Z3 + h, lambda k: zs3.at[h], zr3.at[h, c])
        zr3[h, c] = zs3[h]

    def pass4(h, g0):
        sums = [SUM[:, lane_cols(g0 + k)] if h else jnp.zeros((SUB, LANES), f32) for k in range(GROUPS4)]
        for q in range(part_rows // CHUNK):
            hq = (h * (part_rows // CHUNK) + q) * SUB
            inner = [jnp.zeros((SUB, LANES), f32) for _ in range(GROUPS4)]
            for i in range(h * part_rows + q * CHUNK, h * part_rows + (q + 1) * CHUNK, SUB):
                a = lanes_u[i:i + SUB, :]
                for k in range(GROUPS4):
                    inner[k] = inner[k] + R[i:i + SUB, lane_cols(g0 + k)] * a
            for k in range(GROUPS4):
                sums[k] = sums[k] + inner[k] * MH[hq:hq + SUB, lane_cols(g0 + k)]
        for k in range(GROUPS4):
            if h < PARTS - 1:
                SUM[:, lane_cols(g0 + k)] = sums[k]
            else:
                cs4[pl.ds(g0 + k, 1), :] = jnp.sum(sums[k], axis=0, keepdims=True)

    def scale_rows(h):
        arrived(Z3 + h, zr3.at[h, pl.ds(0, ncol - 1)])
        block = slice(h * part_blocks, (h + 1) * part_blocks)
        u = gm[block, :] / jnp.sum(zr3[h], axis=0)
        row_weights(u, h)
        row_f[block, :] = jnp.log2(u) - row_f[block, :]

    for h in range(PARTS - 1):
        scale_rows(h)

        def pass4_tile(t, carry, h=h):
            pass4(h, t * GROUPS4)
            return carry

        lax.fori_loop(0, groups // GROUPS4, pass4_tile, 0)
    scale_rows(PARTS - 1)

    def pass4_other(j, carry):
        for k in range(SUB // GROUPS4):
            pass4(PARTS - 1, (other + j) * SUB + k * GROUPS4)
        at = tile_rows(other + j)
        send(CORE4 + j, {"row": partner}, cs4.at[at], cr4.at[at])
        return carry

    def pass4_own(j, carry):
        for k in range(SUB // GROUPS4):
            pass4(PARTS - 1, (own + j) * SUB + k * GROUPS4)
        at = tile_rows(own + j)
        mine = tile_rows(j)
        arrived(CORE4 + j, cr4.at[at])
        both = cs4[at, :] + cr4[at, :]
        gs4[mine, :] = both
        ag4[chip, mine, :] = both
        to_chips(CHIP4 + j, gs4.at[mine], ag4.at[chip, mine])
        return carry

    lax.fori_loop(0, half_tiles, pass4_other, 0)
    lax.fori_loop(0, half_tiles, pass4_own, 0)

    arrived(A2, ta.at[pl.ds(0, chips - 1)])
    log_total = jnp.log2(jnp.sum(ta[...], axis=0)[0:1, :])
    for k in range(row_blocks):
        wide = x[k * LANES:(k + 1) * LANES, :].astype(f32)
        half = 0.5 * jnp.sum((wide * wide).T, axis=0, keepdims=True)
        f_out[k:k + 1, :] = half + (row_f[k:k + 1, :] - log_total) * (1.0 / SCALE)
    lanes_u[...] = lanes_u[...] * float(rows * nrow)
    acc_a[...] = jnp.zeros(acc_a.shape, f32)

    for j in range(half_tiles):
        mine = slice(j * SUB, (j + 1) * SUB)
        at = tile_rows(own + j)
        arrived(CHIP4 + j, ag4.at[pl.ds(0, chips - 1), mine])
        col4[at, :] = rm[at, :] / (ref_total * jnp.sum(ag4[:, mine, :], axis=0))
    send(BACK4, {"row": partner}, col4.at[own_groups], col4.at[own_groups])
    arrived(BACK4, col4.at[other_groups])

    n5 = TILE5 // LANES
    share = ROWS5 // ncol

    def pass5(b, carry):
        base = pl.multiple_of(b * ROWS5, ROWS5)
        pulled = jnp.zeros((ROWS5, width), f32)
        for t in range(cols // TILE5):
            low = [[] for _ in range(n5)]
            for q in range(ROWS5 // CHUNK):
                hq = pl.ds(pl.multiple_of(b * (ROWS5 // CHUNK * SUB) + q * SUB, SUB), SUB)
                w = [MH[hq, (t * n5 + k) * LANES:(t * n5 + k + 1) * LANES] * col4[t * n5 + k:t * n5 + k + 1, :]
                     for k in range(n5)]
                for i in range(q * CHUNK, (q + 1) * CHUNK, SUB):
                    at = pl.ds(pl.multiple_of(base + i, SUB), SUB)
                    a = lanes_u[at, :]
                    mass = acc_a[at, :]
                    for k in range(n5):
                        p = (R[at, (t * n5 + k) * LANES:(t * n5 + k + 1) * LANES] * w[k]) * a
                        mass = mass + p
                        low[k].append(p)
                    acc_a[at, :] = mass
            plan_low = jnp.concatenate(
                [jnp.concatenate(v, axis=0).astype(jnp.bfloat16) for v in low], axis=1
            )
            pulled = pulled + jnp.dot(plan_low, y[t * TILE5:(t + 1) * TILE5, :], preferred_element_type=f32)
        whole = pl.ds(base, ROWS5)
        mass_row = jnp.sum(acc_a[whole, :], axis=1, keepdims=True)
        part[whole, :] = mass_row * x[whole, :].astype(f32) - pulled
        to_cols(
            RS + b,
            lambda k: part.at[pl.ds(pl.multiple_of(base + k * share, share), share)],
            pr5.at[b, c],
        )
        pr5[b, c] = part[pl.ds(pl.multiple_of(base + c * share, share), share), :]
        return carry

    lax.fori_loop(0, rows // ROWS5, pass5, 0)

    for j in range(tiles):
        at = slice(j * SUB, (j + 1) * SUB)
        g_out[at, :] = (
            (2.0 * log_total + jnp.log2(rm[at, :]) - col2[at, :]) + jnp.log2(col4[at, :])
        ) * (1.0 / SCALE)

    def finish(b, carry):
        mine = pl.ds(pl.multiple_of(b * ROWS5 + c * share, share), share)
        arrived(RS + b, pr5.at[b, pl.ds(0, ncol - 1)])
        done[mine, :] = jnp.sum(pr5[b], axis=0)
        to_cols(AG + b, lambda k: done.at[mine], done.at[mine])
        return carry

    lax.fori_loop(0, rows // ROWS5, finish, 0)
    for b in range(rows // ROWS5):
        arrived(AG + b, done.at[pl.ds(0, ROWS5 - share)])
    grad_out[...] = done[...]

    for h in range(PARTS):
        left(Z1 + h, zr1.at[h, pl.ds(0, ncol - 1)])
        left(Z3 + h, zr3.at[h, pl.ds(0, ncol - 1)])
    left(A1, ra)
    left(A2, ta.at[pl.ds(0, chips - 1)])
    for j in range(half_tiles):
        mine = slice(j * SUB, (j + 1) * SUB)
        left(CORE2 + j, cs2.at[mine])
        left(CORE4 + j, cs4.at[mine])
        left(CHIP2 + j, ag2.at[pl.ds(0, chips - 1), mine])
        left(CHIP4 + j, ag4.at[pl.ds(0, chips - 1), mine])
    left(BACK2, col2.at[own_groups])
    left(BACK4, col4.at[own_groups])
    for b in range(rows // ROWS5):
        left(RS + b, pr5.at[b, pl.ds(0, ncol - 1)])
        left(AG + b, done.at[pl.ds(0, ROWS5 - share)])


def local(nrow, ncol, gen_points, ref_points, gen_mass, ref_mass):
    rows, width = gen_points.shape
    cols = ref_points.shape[0]
    row_blocks = rows // LANES
    groups = cols // LANES
    chunks = rows // CHUNK
    chips = nrow // 2
    vmem = pl.BlockSpec(memory_space=pltpu.VMEM)

    def buf(*shape):
        return pltpu.VMEM(shape, f32)

    def body(*refs):
        kernel(nrow, ncol, *refs)

    f, g, grad = pl.pallas_call(
        body,
        out_shape=(
            jax.ShapeDtypeStruct((row_blocks, LANES), f32),
            jax.ShapeDtypeStruct((groups, LANES), f32),
            jax.ShapeDtypeStruct((rows, width), f32),
        ),
        in_specs=[vmem] * 4,
        out_specs=(vmem, vmem, vmem),
        scratch_shapes=[
            buf(rows, cols), buf(chunks * SUB, cols), buf(SUB, cols), buf(SUB, cols), buf(groups, LANES),
            buf(rows, LANES), buf(rows, LANES), buf(rows, LANES), buf(row_blocks, LANES),
            buf(SUB, LANES), buf(SUB, LANES), buf(SUB, LANES), buf(chips, SUB, LANES),
            buf(PARTS, SUB, LANES), buf(PARTS, ncol, SUB, LANES),
            buf(PARTS, row_blocks // PARTS, LANES), buf(PARTS, ncol, row_blocks // PARTS, LANES),
            buf(groups, LANES), buf(groups, LANES), buf(groups // 2, LANES),
            buf(chips, groups // 2, LANES), buf(groups, LANES),
            buf(groups, LANES), buf(groups, LANES), buf(groups // 2, LANES),
            buf(chips, groups // 2, LANES), buf(groups, LANES),
            buf(SUB, width), buf(rows, width),
            buf(rows // ROWS5, ncol, ROWS5 // ncol, width), buf(rows, width),
            pltpu.SemaphoreType.DMA((32,)),
            pltpu.SemaphoreType.DMA((32,)),
        ],
        compiler_params=pltpu.CompilerParams(
            collective_id=0, has_side_effects=True, vmem_limit_bytes=56 * 2**20
        ),
        name="sinkhorn",
    )(gen_points, ref_points, gen_mass.reshape(row_blocks, LANES), ref_mass.reshape(groups, LANES))
    return f.reshape(rows), g.reshape(cols), grad


def solution(mesh):
    nrow, ncol = mesh.shape["row"], mesh.shape["col"]

    def run(*args):
        return local(nrow, ncol, *args)

    return jax.shard_map(
        run,
        mesh=mesh,
        in_specs=(P("row", None), P("col", None), P("row"), P("col")),
        out_specs=(P("row"), P("col"), P("row", None)),
        check_vma=False,
    )
```

time: 82.6 us -> 70.5 us (0.85)
  Pallas kernels: 77.4 us -> 65.3 us
    pallas_call x1, Pallas kernels: 77.4 us -> 65.3 us  [local(): pl.pallas_call(body, out_shape=(jax.ShapeDtypeStruct((row_blocks, LANES),...]
where the time goes in v2:
time: 70.5 us; the launch traced here: 70.2 us
  Pallas kernels  65.3 us (93%)
  local copies, waits for them, and re-layouts  4.3 us (6%)
    pallas_call x1, Pallas kernels, local(): pl.pallas_call(body, out_shape=(jax.ShapeDtypeStruct((row_blocks, LANES),...  65.3 us
    unnamed x3, local copies, waits for them, and re-layouts  4.3 us

profile of v2, /device:TPU:1, one launch (start us, length us, event | category | flops | bytes accessed | tf_op | source)
XLA Modules:
  0.0 70.2 jit_solution(7096102373018524128)
XLA Ops:
  0.6 65.3 %sinkhorn.1 = (f32[4,128]{1,0:T(4,128)}, f32[64,128]{1,0:T(8,128)}, f32[512,128]{1,0:T(8,128)}) custom-call(bf16[512,128]{1,0:T(8,128)(2,1)} %refs_0_.1, bf16[8192,128]{1,0:T(8,128)(2,1)} %refs_1_.1, f32[4,128]{1,0:T(4,128)} %bitcast.6, f32[64,128]{1,0:T(8,128)} %bitcast.4), custom_call_target="tpu_custom_call" | custom-call | tf_op jit(solution)/shard_map/sinkhorn/pallas_call | solution.py:489
  65.9 1.3 %copy.10 = f32[512]{0:T(512)} copy(f32[512]{0:T(512)} %bitcast.7) | data formatting | bytes 4096
  67.2 1.4 %copy.11 = f32[8192]{0:T(1024)} copy(f32[8192]{0:T(1024)} %bitcast.5) | data formatting | bytes 65536
  68.6 1.7 %copy.12 = f32[512,128]{1,0:T(8,128)} copy(f32[512,128]{1,0:T(8,128)} %get-tuple-element.14) | data formatting | bytes 524288

commit v3 on v2

v3 whole, which is shorter than its diff:
```python
import math

import jax
import jax.numpy as jnp
from jax import lax
from jax.experimental import pallas as pl
from jax.experimental.pallas import tpu as pltpu
from jax.sharding import PartitionSpec as P

smoothing_epsilon = 0.05
SCALE = 1.0 / (smoothing_epsilon * math.log(2.0))
LANES = 128
SUB = 8
LOWEST = -3.0e38
f32 = jnp.float32
MESH = pl.DeviceIdType.MESH

CHUNK = 64
TILE0 = 2048
TILE1 = 4096
TILE2 = 4096
WIDE = 16
GROUPS3 = 16
GROUPS4 = 4
TILE5 = 2048
ROWS5 = 128
PARTS = 4
HALVES = 2


def scores(a, b):
    return lax.dot_general(a, b, (((1,), (1,)), ((), ())), preferred_element_type=f32)


def lane_cols(group):
    return pl.ds(pl.multiple_of(group * LANES, LANES), LANES)


def tile_rows(t):
    return pl.ds(pl.multiple_of(t * SUB, SUB), SUB)


def total(v):
    return jnp.sum(jnp.sum(v, axis=0, keepdims=True), axis=1, keepdims=True)


def log_sum(v):
    top = jnp.max(v, axis=0)
    return top + jnp.log2(jnp.sum(jnp.exp2(v - top[None]), axis=0))


def kernel(
    nrow, ncol, x, y_hbm, gm, rm, f_out, g_out, grad_out,
    y, R, MH, W, TOP, SUM, beta, acc_a, acc_b, lanes_u, row_f,
    sa, ra, ca, ta, zs1, zr1, zs3, zr3,
    cs2, cr2, gs2, ag2, col2, colw, cs4, cr4, gs4, ag4, col4,
    part, pr5, done, send_sem, recv_sem, load_sem,
):
    rows, width = x.shape
    cols = y.shape[0]
    loads = [
        pltpu.make_async_copy(
            y_hbm.at[pl.ds(t * TILE0, TILE0)], y.at[pl.ds(t * TILE0, TILE0)], load_sem.at[t]
        )
        for t in range(cols // TILE0)
    ]
    for load in loads:
        load.start()
    row_blocks = rows // LANES
    groups = cols // LANES
    tiles = groups // SUB
    half_tiles = tiles // 2
    half_groups = groups // 2
    chips = nrow // 2
    part_rows = rows // PARTS
    part_chunks = part_rows // CHUNK
    half_rows = rows // HALVES
    half_blocks = half_rows // LANES
    half_chunks = half_rows // CHUNK
    r = lax.axis_index("row")
    c = lax.axis_index("col")
    core = lax.rem(r, 2)
    chip = r // 2
    partner = 2 * chip + (1 - core)
    own = core * half_tiles
    other = (1 - core) * half_tiles

    def chip_peer(s):
        return lax.rem(r + 2 * s, nrow)

    def col_peer(s):
        return lax.rem(c + s, ncol)

    barrier = pltpu.get_barrier_semaphore()

    def greet_row(s, carry):
        pl.semaphore_signal(barrier, inc=1, device_id={"row": chip_peer(s)}, device_id_type=MESH)
        return carry

    def greet_col(s, carry):
        pl.semaphore_signal(barrier, inc=1, device_id={"col": col_peer(s)}, device_id_type=MESH)
        return carry

    pl.semaphore_signal(barrier, inc=1, device_id={"row": partner}, device_id_type=MESH)
    lax.fori_loop(1, chips, greet_row, 0)
    lax.fori_loop(1, ncol, greet_col, 0)

    def send(phase, device, source, target):
        pltpu.make_async_remote_copy(
            src_ref=source,
            dst_ref=target,
            send_sem=send_sem.at[phase],
            recv_sem=recv_sem.at[phase],
            device_id=device,
            device_id_type=MESH,
        ).start()

    def to_chips(phase, source, target):
        def one(s, carry):
            send(phase, {"row": chip_peer(s)}, source, target)
            return carry

        lax.fori_loop(1, chips, one, 0)

    def to_cols(phase, source, target):
        def one(s, carry):
            k = col_peer(s)
            send(phase, {"col": k}, source(k), target)
            return carry

        lax.fori_loop(1, ncol, one, 0)

    def arrived(phase, whole):
        pltpu.make_async_copy(whole, whole, recv_sem.at[phase]).wait()

    def left(phase, whole):
        pltpu.make_async_copy(whole, whole, send_sem.at[phase]).wait()

    Z1, Z3, CORE2, CHIP2, BACK2, CORE4, CHIP4, BACK4, A1, A2, RS, AG = (
        0, 4, 6, 10, 14, 15, 19, 23, 24, 25, 26, 34,
    )

    log_ref = jnp.log2(rm[...])
    beta[...] = log_ref
    zs1[...] = jnp.broadcast_to(total(rm[...])[None], zs1.shape)
    sa[...] = jnp.broadcast_to(total(gm[...]), sa.shape)
    acc_a[...] = jnp.full(acc_a.shape, LOWEST, f32)
    acc_b[...] = jnp.zeros(acc_b.shape, f32)
    TOP[...] = jnp.full(TOP.shape, LOWEST, f32)
    SUM[...] = jnp.zeros(SUM.shape, f32)

    def pass1(base, block, g0):
        rows_now = pl.ds(pl.multiple_of(base, part_rows), part_rows)
        tops, sums = acc_a.at[rows_now], acc_b.at[rows_now]
        for b in range(0, block.shape[1] // LANES, WIDE):
            bias = [beta[pl.ds(g0 + b + k, 1), :] for k in range(WIDE)]
            for i in range(0, part_rows, SUB):
                at = slice(i, i + SUB)
                e = [block[i:i + SUB, (b + k) * LANES:(b + k + 1) * LANES] * SCALE + bias[k] for k in range(WIDE)]
                old = tops[at, :]
                top = e[0]
                for v in e[1:]:
                    top = jnp.maximum(top, v)
                top = jnp.maximum(top, old)
                total_s = sums[at, :] * jnp.exp2(old - top)
                for v in e:
                    total_s = total_s + jnp.exp2(v - top)
                tops[at, :] = top
                sums[at, :] = total_s

    def report(h):
        o = pl.ds(pl.multiple_of(h * part_rows, part_rows), LANES)
        v = (acc_a[o, :] + jnp.log2(acc_b[o, :])).T
        top = jnp.max(v, axis=0, keepdims=True)
        zs1[h, 0:1, :] = top + jnp.log2(jnp.sum(jnp.exp2(v - top), axis=0, keepdims=True))

    def tell(h):
        to_cols(Z1 + h, lambda k: zs1.at[h], zr1.at[h, c])
        zr1[h, c] = zs1[h]

    n0 = TILE0 // LANES
    for t in range(cols // TILE0):
        loads[t].wait()
        points = y[t * TILE0:(t + 1) * TILE0, :]
        block = scores(x[0:part_rows, :], points)
        for k in range(n0):
            wide = points[k * LANES:(k + 1) * LANES, :].astype(f32)
            half = jnp.sum((wide * wide).T, axis=0, keepdims=True)
            g = t * n0 + k
            beta[g:g + 1, :] = beta[g:g + 1, :] - (0.5 * SCALE) * half
        pass1(0, block, t * n0)
    report(0)
    pl.semaphore_wait(barrier, chips + ncol - 1)
    tell(0)
    send(A1, {"row": partner}, sa, ra)

    n1 = TILE1 // LANES

    def pass1_part(h, carry):
        base = pl.multiple_of(h * part_rows, part_rows)

        def tile(t, carry):
            block = scores(x[pl.ds(base, part_rows), :], y[pl.ds(pl.multiple_of(t * TILE1, TILE1), TILE1), :])
            pass1(base, block, t * n1)
            return carry

        lax.fori_loop(0, cols // TILE1, tile, 0)
        report(h)
        tell(h)
        return carry

    lax.fori_loop(1, PARTS, pass1_part, 0)

    n2 = TILE2 // LANES
    t2 = n2 // SUB

    def spread(at, v):
        lanes_u[at, :] = jnp.broadcast_to(v, (LANES, LANES)).T

    def pass2(h, g0, last):
        base = pl.multiple_of(h * part_rows, part_rows)
        here = pl.ds(pl.multiple_of(g0 * LANES, TILE2), TILE2)
        block = scores(x[pl.ds(base, part_rows), :], y[here, :])
        powers = R.at[pl.ds(base, part_rows), here]
        u = lanes_u.at[pl.ds(base, part_rows)]
        marks = MH.at[pl.ds(pl.multiple_of(h * (part_chunks * SUB), SUB), part_chunks * SUB), here]
        top_now, sum_now = TOP.at[:, here], SUM.at[:, here]
        for b in range(0, n2, WIDE):
            cols_of = [slice(k * LANES, (k + 1) * LANES) for k in range(b, b + WIDE)]
            tops = [top_now[:, at] for at in cols_of]
            sums = [sum_now[:, at] for at in cols_of]
            bias = [beta[pl.ds(g0 + k, 1), :] for k in range(b, b + WIDE)]
            for j, at in enumerate(cols_of):
                top, s = tops[j], sums[j]
                for q in range(part_chunks):
                    span = range(q * CHUNK, (q + 1) * CHUNK, SUB)
                    e = [block[i:i + SUB, at] * SCALE + u[i:i + SUB, :] for i in span]
                    old = top
                    for v in e:
                        top = jnp.maximum(top, v)
                    s = s * jnp.exp2(old - top)
                    for i, v in zip(span, e):
                        z = jnp.exp2(v - top)
                        powers[i:i + SUB, at] = z
                        s = s + z
                    marks[q * SUB:(q + 1) * SUB, at] = top + bias[j]
                tops[j], sums[j] = top, s
            for j, at in enumerate(cols_of):
                if last:
                    best = jnp.max(tops[j], axis=0, keepdims=True)
                    s = jnp.sum(sums[j] * jnp.exp2(tops[j] - best), axis=0, keepdims=True)
                    cs2[pl.ds(g0 + b + j, 1), :] = best + jnp.log2(s) + bias[j]
                else:
                    top_now[:, at] = tops[j]
                    sum_now[:, at] = sums[j]

    def log_of_rows(h):
        arrived(Z1 + h, zr1.at[h, pl.ds(0, ncol - 1)])
        v = zr1[h]
        ref_total = jnp.sum(v, axis=0)[1:2, :]
        row_lse = log_sum(v)[0:1, :] - jnp.log2(ref_total)
        row_f[pl.ds(h, 1), :] = row_lse
        spread(pl.ds(pl.multiple_of(h * part_rows, part_rows), part_rows), jnp.log2(gm[pl.ds(h, 1), :]) - row_lse)
        return ref_total

    def pass2_part(h, carry):
        log_of_rows(h)

        def tile(t, carry):
            pass2(h, t * n2, False)
            return carry

        lax.fori_loop(0, groups // n2, tile, 0)
        return carry

    lax.fori_loop(0, PARTS - 1, pass2_part, 0)
    arrived(A1, ra)
    ca[...] = sa[...] + ra[...]
    to_chips(A2, ca, ta.at[chip])
    ta[chip] = ca[...]
    ref_total = log_of_rows(PARTS - 1)
    shares = jnp.log2(rm[...]) - jnp.log2(ref_total)

    def pass2_other(t, carry):
        g0 = other * SUB + t * n2
        pass2(PARTS - 1, g0, True)
        for j in range(t2):
            at = tile_rows(other + t * t2 + j)
            send(CORE2 + t * t2 + j, {"row": partner}, cs2.at[at], cr2.at[at])
        return carry

    def pass2_own(t, carry):
        g0 = own * SUB + t * n2
        pass2(PARTS - 1, g0, True)
        for j in range(t2):
            at = tile_rows(own + t * t2 + j)
            mine = tile_rows(t * t2 + j)
            arrived(CORE2 + t * t2 + j, cr2.at[at])
            a, b = cs2[at, :], cr2[at, :]
            top = jnp.maximum(a, b)
            both = top + jnp.log2(jnp.exp2(a - top) + jnp.exp2(b - top))
            gs2[mine, :] = both
            ag2[chip, mine, :] = both
            to_chips(CHIP2 + t * t2 + j, gs2.at[mine], ag2.at[chip, mine])
        return carry

    lax.fori_loop(0, half_groups // n2, pass2_other, 0)
    lax.fori_loop(0, half_groups // n2, pass2_own, 0)

    for j in range(half_tiles):
        mine = slice(j * SUB, (j + 1) * SUB)
        arrived(CHIP2 + j, ag2.at[pl.ds(0, chips - 1), mine])
        col2[tile_rows(own + j), :] = log_sum(ag2[:, mine, :])
    own_groups = pl.ds(pl.multiple_of(own * SUB, SUB), half_groups)
    other_groups = pl.ds(pl.multiple_of(other * SUB, SUB), half_groups)
    send(BACK2, {"row": partner}, col2.at[own_groups], col2.at[own_groups])
    colw[...] = -shares

    def weigh(half):
        colw[half, :] = col2[half, :] + colw[half, :]

    def pass3(first, h):
        def tile(t, carry):
            g0 = first * SUB + t * GROUPS3
            here = pl.ds(pl.multiple_of(g0 * LANES, GROUPS3 * LANES), GROUPS3 * LANES)
            powers, marks, weights = R.at[:, here], MH.at[:, here], W.at[:, here]
            cols_of = [slice(k * LANES, (k + 1) * LANES) for k in range(GROUPS3)]
            shift = [colw[pl.ds(g0 + k, 1), :] for k in range(GROUPS3)]
            for q in range(half_chunks):
                hq = (h * half_chunks + q) * SUB
                w = []
                for k, at in enumerate(cols_of):
                    v = jnp.exp2(marks[hq:hq + SUB, at] - shift[k])
                    weights[hq:hq + SUB, at] = v
                    w.append(v)
                for i in range(h * half_rows + q * CHUNK, h * half_rows + (q + 1) * CHUNK, SUB):
                    even = acc_a[i:i + SUB, :]
                    odd = jnp.zeros((SUB, LANES), f32)
                    for k, at in enumerate(cols_of):
                        v = powers[i:i + SUB, at] * w[k]
                        if k % 2:
                            odd = odd + v
                        else:
                            even = even + v
                    acc_a[i:i + SUB, :] = even + odd
            return carry

        lax.fori_loop(0, half_groups // GROUPS3, tile, 0)

    acc_a[...] = jnp.zeros(acc_a.shape, f32)
    weigh(own_groups)
    for h in range(HALVES):
        pass3(own, h)
    arrived(BACK2, col2.at[other_groups])
    weigh(other_groups)
    for h in range(HALVES):
        pass3(other, h)
        for k in range(half_blocks):
            o = (h * half_blocks + k) * LANES
            zs3[h, k:k + 1, :] = jnp.sum(acc_a[o:o + LANES, :].T, axis=0, keepdims=True)
        to_cols(Z3 + h, lambda k: zs3.at[h], zr3.at[h, c])
        zr3[h, c] = zs3[h]

    def pass4(h, g0):
        here = pl.ds(pl.multiple_of(g0 * LANES, GROUPS4 * LANES), GROUPS4 * LANES)
        powers, weights, partial = R.at[:, here], W.at[:, here], SUM.at[:, here]
        cols_of = [slice(k * LANES, (k + 1) * LANES) for k in range(GROUPS4)]
        sums = [partial[:, at] if h else jnp.zeros((SUB, LANES), f32) for at in cols_of]
        for q in range(half_chunks):
            hq = (h * half_chunks + q) * SUB
            inner = [jnp.zeros((SUB, LANES), f32) for _ in range(GROUPS4)]
            for i in range(h * half_rows + q * CHUNK, h * half_rows + (q + 1) * CHUNK, SUB):
                a = lanes_u[i:i + SUB, :]
                for k, at in enumerate(cols_of):
                    inner[k] = inner[k] + powers[i:i + SUB, at] * a
            for k, at in enumerate(cols_of):
                sums[k] = sums[k] + inner[k] * weights[hq:hq + SUB, at]
        for k, at in enumerate(cols_of):
            if h < HALVES - 1:
                partial[:, at] = sums[k]
            else:
                cs4[pl.ds(g0 + k, 1), :] = jnp.sum(sums[k], axis=0, keepdims=True)

    def scale_rows(h):
        arrived(Z3 + h, zr3.at[h, pl.ds(0, ncol - 1)])
        block = slice(h * half_blocks, (h + 1) * half_blocks)
        u = gm[block, :] / jnp.sum(zr3[h], axis=0)
        for k in range(half_blocks):
            o = (h * half_blocks + k) * LANES
            spread(slice(o, o + LANES), u[k:k + 1, :])
        row_f[block, :] = jnp.log2(u) - row_f[block, :]

    for h in range(HALVES - 1):
        scale_rows(h)

        def pass4_tile(t, carry, h=h):
            pass4(h, t * GROUPS4)
            return carry

        lax.fori_loop(0, groups // GROUPS4, pass4_tile, 0)
    scale_rows(HALVES - 1)

    def pass4_other(j, carry):
        for k in range(SUB // GROUPS4):
            pass4(HALVES - 1, (other + j) * SUB + k * GROUPS4)
        at = tile_rows(other + j)
        send(CORE4 + j, {"row": partner}, cs4.at[at], cr4.at[at])
        return carry

    def pass4_own(j, carry):
        for k in range(SUB // GROUPS4):
            pass4(HALVES - 1, (own + j) * SUB + k * GROUPS4)
        at = tile_rows(own + j)
        mine = tile_rows(j)
        arrived(CORE4 + j, cr4.at[at])
        both = cs4[at, :] + cr4[at, :]
        gs4[mine, :] = both
        ag4[chip, mine, :] = both
        to_chips(CHIP4 + j, gs4.at[mine], ag4.at[chip, mine])
        return carry

    lax.fori_loop(0, half_tiles, pass4_other, 0)
    lax.fori_loop(0, half_tiles, pass4_own, 0)

    arrived(A2, ta.at[pl.ds(0, chips - 1)])
    log_total = jnp.log2(jnp.sum(ta[...], axis=0)[0:1, :])
    for k in range(row_blocks):
        wide = x[k * LANES:(k + 1) * LANES, :].astype(f32)
        half = 0.5 * jnp.sum((wide * wide).T, axis=0, keepdims=True)
        f_out[k:k + 1, :] = half + (row_f[k:k + 1, :] - log_total) * (1.0 / SCALE)
    lanes_u[...] = lanes_u[...] * float(rows * nrow)
    acc_a[...] = jnp.zeros(acc_a.shape, f32)

    for j in range(half_tiles):
        mine = slice(j * SUB, (j + 1) * SUB)
        at = tile_rows(own + j)
        arrived(CHIP4 + j, ag4.at[pl.ds(0, chips - 1), mine])
        col4[at, :] = rm[at, :] / (ref_total * jnp.sum(ag4[:, mine, :], axis=0))
    send(BACK4, {"row": partner}, col4.at[own_groups], col4.at[own_groups])
    arrived(BACK4, col4.at[other_groups])

    n5 = TILE5 // LANES
    share = ROWS5 // ncol

    def pass5(b, carry):
        base = pl.multiple_of(b * ROWS5, ROWS5)
        whole = pl.ds(base, ROWS5)
        powers, u, masses = R.at[whole], lanes_u.at[whole], acc_a.at[whole]
        chunks_here = ROWS5 // CHUNK
        weights = W.at[pl.ds(pl.multiple_of(b * (chunks_here * SUB), SUB), chunks_here * SUB)]
        pulled = jnp.zeros((ROWS5, width), f32)
        for t in range(cols // TILE5):
            low = [[] for _ in range(n5)]
            for q in range(ROWS5 // CHUNK):
                hq = slice(q * SUB, (q + 1) * SUB)
                w = [weights[hq, (t * n5 + k) * LANES:(t * n5 + k + 1) * LANES] * col4[t * n5 + k:t * n5 + k + 1, :]
                     for k in range(n5)]
                for i in range(q * CHUNK, (q + 1) * CHUNK, SUB):
                    at = slice(i, i + SUB)
                    a = u[at, :]
                    mass = masses[at, :]
                    for k in range(n5):
                        p = (powers[at, (t * n5 + k) * LANES:(t * n5 + k + 1) * LANES] * w[k]) * a
                        mass = mass + p
                        low[k].append(p)
                    masses[at, :] = mass
            plan_low = jnp.concatenate(
                [jnp.concatenate(v, axis=0).astype(jnp.bfloat16) for v in low], axis=1
            )
            pulled = pulled + jnp.dot(plan_low, y[t * TILE5:(t + 1) * TILE5, :], preferred_element_type=f32)
        mass_row = jnp.sum(masses[...], axis=1, keepdims=True)
        part[whole, :] = mass_row * x[whole, :].astype(f32) - pulled
        to_cols(
            RS + b,
            lambda k: part.at[pl.ds(pl.multiple_of(base + k * share, share), share)],
            pr5.at[b, c],
        )
        pr5[b, c] = part[pl.ds(pl.multiple_of(base + c * share, share), share), :]
        return carry

    lax.fori_loop(0, rows // ROWS5, pass5, 0)

    for j in range(tiles):
        at = slice(j * SUB, (j + 1) * SUB)
        g_out[at, :] = (
            (2.0 * log_total + jnp.log2(rm[at, :]) - col2[at, :]) + jnp.log2(col4[at, :])
        ) * (1.0 / SCALE)

    def finish(b, carry):
        mine = pl.ds(pl.multiple_of(b * ROWS5 + c * share, share), share)
        arrived(RS + b, pr5.at[b, pl.ds(0, ncol - 1)])
        done[mine, :] = jnp.sum(pr5[b], axis=0)
        to_cols(AG + b, lambda k: done.at[mine], done.at[mine])
        return carry

    lax.fori_loop(0, rows // ROWS5, finish, 0)
    for b in range(rows // ROWS5):
        arrived(AG + b, done.at[pl.ds(0, ROWS5 - share)])
    grad_out[...] = done[...]

    for h in range(PARTS):
        left(Z1 + h, zr1.at[h, pl.ds(0, ncol - 1)])
    for h in range(HALVES):
        left(Z3 + h, zr3.at[h, pl.ds(0, ncol - 1)])
    left(A1, ra)
    left(A2, ta.at[pl.ds(0, chips - 1)])
    for j in range(half_tiles):
        mine = slice(j * SUB, (j + 1) * SUB)
        left(CORE2 + j, cs2.at[mine])
        left(CORE4 + j, cs4.at[mine])
        left(CHIP2 + j, ag2.at[pl.ds(0, chips - 1), mine])
        left(CHIP4 + j, ag4.at[pl.ds(0, chips - 1), mine])
    left(BACK2, col2.at[own_groups])
    left(BACK4, col4.at[own_groups])
    for b in range(rows // ROWS5):
        left(RS + b, pr5.at[b, pl.ds(0, ncol - 1)])
        left(AG + b, done.at[pl.ds(0, ROWS5 - share)])


def move(f, g, grad, f_out, g_out, grad_out):
    f_out[...] = f[...]
    g_out[...] = g[...]
    grad_out[...] = grad[...]


def hand_on(*arrays):
    vmem = pl.BlockSpec(memory_space=pltpu.VMEM)
    return pl.pallas_call(
        move,
        out_shape=tuple(jax.ShapeDtypeStruct(a.shape, a.dtype) for a in arrays),
        in_specs=[vmem] * 3,
        out_specs=(vmem,) * 3,
        name="hand_on",
    )(*arrays)


def local(nrow, ncol, gen_points, ref_points, gen_mass, ref_mass):
    rows, width = gen_points.shape
    cols = ref_points.shape[0]
    row_blocks = rows // LANES
    groups = cols // LANES
    chunks = rows // CHUNK
    chips = nrow // 2
    vmem = pl.BlockSpec(memory_space=pltpu.VMEM)
    anywhere = pl.BlockSpec(memory_space=pl.ANY)

    def buf(*shape):
        return pltpu.VMEM(shape, f32)

    def body(*refs):
        kernel(nrow, ncol, *refs)

    f, g, grad = pl.pallas_call(
        body,
        out_shape=(
            jax.ShapeDtypeStruct((row_blocks, LANES), f32),
            jax.ShapeDtypeStruct((groups, LANES), f32),
            jax.ShapeDtypeStruct((rows, width), f32),
        ),
        in_specs=[vmem, anywhere, vmem, vmem],
        out_specs=(vmem, vmem, vmem),
        scratch_shapes=[
            pltpu.VMEM((cols, width), ref_points.dtype), buf(rows, cols), buf(chunks * SUB, cols), buf(chunks * SUB, cols), buf(SUB, cols), buf(SUB, cols), buf(groups, LANES),
            buf(rows, LANES), buf(rows, LANES), buf(rows, LANES), buf(row_blocks, LANES),
            buf(SUB, LANES), buf(SUB, LANES), buf(SUB, LANES), buf(chips, SUB, LANES),
            buf(PARTS, SUB, LANES), buf(PARTS, ncol, SUB, LANES),
            buf(HALVES, row_blocks // HALVES, LANES), buf(HALVES, ncol, row_blocks // HALVES, LANES),
            buf(groups, LANES), buf(groups, LANES), buf(groups // 2, LANES),
            buf(chips, groups // 2, LANES), buf(groups, LANES), buf(groups, LANES),
            buf(groups, LANES), buf(groups, LANES), buf(groups // 2, LANES),
            buf(chips, groups // 2, LANES), buf(groups, LANES),
            buf(rows, width),
            buf(rows // ROWS5, ncol, ROWS5 // ncol, width), buf(rows, width),
            pltpu.SemaphoreType.DMA((42,)),
            pltpu.SemaphoreType.DMA((42,)),
            pltpu.SemaphoreType.DMA((cols // TILE0,)),
        ],
        compiler_params=pltpu.CompilerParams(
            collective_id=0, has_side_effects=True, vmem_limit_bytes=56 * 2**20
        ),
        name="sinkhorn",
    )(gen_points, ref_points, gen_mass.reshape(row_blocks, LANES), ref_mass.reshape(groups, LANES))
    f, g, grad = hand_on(f, g, grad)
    return f.reshape(rows), g.reshape(cols), grad


def solution(mesh):
    nrow, ncol = mesh.shape["row"], mesh.shape["col"]

    def run(*args):
        return local(nrow, ncol, *args)

    return jax.shard_map(
        run,
        mesh=mesh,
        in_specs=(P("row", None), P("col", None), P("row"), P("col")),
        out_specs=(P("row"), P("col"), P("row", None)),
        check_vma=False,
    )
```

time: 70.5 us -> 63.8 us (0.905)
  local copies, waits for them, and re-layouts: 4.3 us -> 0 us
  Pallas kernels: 65.3 us -> 63 us
    unnamed x3 -> x0, local copies, waits for them, and re-layouts: 4.3 us -> none
    pallas_call x1, Pallas kernels: 65.3 us -> 61.3 us  [local(): pl.pallas_call(body, out_shape=(jax.ShapeDtypeStruct((row_blocks, LANES),...]
    pallas_call x0 -> x1, Pallas kernels: none -> 1.7 us  [hand_on(): pl.pallas_call(move, out_shape=tuple((jax.ShapeDtypeStruct(a.shape, a.dty...]
where the time goes in v3:
time: 63.8 us; the launch traced here: 63.7 us
  Pallas kernels  63 us (99%)
  between operations  0.64 us (1%)
    pallas_call x1, Pallas kernels, local(): pl.pallas_call(body, out_shape=(jax.ShapeDtypeStruct((row_blocks, LANES),...  61.3 us
    pallas_call x1, Pallas kernels, hand_on(): pl.pallas_call(move, out_shape=tuple((jax.ShapeDtypeStruct(a.shape, a.dty...  1.7 us

profile of v3, /device:TPU:1, one launch (start us, length us, event | category | flops | bytes accessed | tf_op | source)
XLA Modules:
  0.0 63.7 jit_solution(16067976179050237186)
XLA Ops:
  0.6 61.3 %sinkhorn.1 = (f32[4,128]{1,0:T(4,128)}, f32[64,128]{1,0:T(8,128)}, f32[512,128]{1,0:T(8,128)}) custom-call(bf16[512,128]{1,0:T(8,128)(2,1)} %refs_0_.1, bf16[8192,128]{1,0:T(8,128)(2,1)} %refs_1_.1, f32[4,128]{1,0:T(4,128)} %bitcast.5, f32[64,128]{1,0:T(8,128)} %bitcast.4), custom_call_target="tpu_custom_call" | custom-call | tf_op jit(solution)/shard_map/sinkhorn/pallas_call | solution.py:553
  62.0 1.7 %hand_on.1 = (f32[4,128]{1,0:T(4,128)}, f32[64,128]{1,0:T(8,128)}, f32[512,128]{1,0:T(8,128)}) custom-call(f32[4,128]{1,0:T(4,128)} %get-tuple-element.9.f, f32[64,128]{1,0:T(8,128)} %get-tuple-element.10.g, f32[512,128]{1,0:T(8,128)} %get-tuple-element.11.grad), custom_call_target="tpu_custom_call" | custom-call | tf_op jit(solution)/shard_map/hand_on/pallas_call | solution.py:528

commit v4 on v3

--- a/solution.py
+++ b/solution.py
@@ -91,6 +91,13 @@
     def col_peer(s):
         return lax.rem(c + s, ncol)
 
+    col_order = sorted(range(1, ncol), key=lambda s: -min(s, ncol - s))
+    side = math.isqrt(chips)
+    chip_order = sorted(
+        range(1, chips),
+        key=lambda s: -(min(s // side, side - s // side) + min(s % side, side - s % side)),
+    )
+
     barrier = pltpu.get_barrier_semaphore()
 
     def greet_row(s, carry):
@@ -120,7 +127,8 @@
             send(phase, {"row": chip_peer(s)}, source, target)
             return carry
 
-        lax.fori_loop(1, chips, one, 0)
+        for s in chip_order:
+            one(s, 0)
 
     def to_cols(phase, source, target):
         def one(s, carry):
@@ -128,7 +136,8 @@
             send(phase, {"col": k}, source(k), target)
             return carry
 
-        lax.fori_loop(1, ncol, one, 0)
+        for s in col_order:
+            one(s, 0)
 
     def arrived(phase, whole):
         pltpu.make_async_copy(whole, whole, recv_sem.at[phase]).wait()
@@ -204,7 +213,7 @@
             pass1(base, block, t * n1)
             return carry
 
-        lax.fori_loop(0, cols // TILE1, tile, 0)
+        lax.fori_loop(0, cols // TILE1, tile, 0, unroll=True)
         report(h)
         tell(h)
         return carry
@@ -270,7 +279,7 @@
             pass2(h, t * n2, False)
             return carry
 
-        lax.fori_loop(0, groups // n2, tile, 0)
+        lax.fori_loop(0, groups // n2, tile, 0, unroll=True)
         return carry
 
     lax.fori_loop(0, PARTS - 1, pass2_part, 0)

time: 63.8 us -> 63.5 us (level)
  no operation moved by 1% of the time
where the time goes in v4:
time: 63.5 us; the launch traced here: 63.3 us
  Pallas kernels  62.7 us (99%)
  between operations  0.64 us (1%)
    pallas_call x1, Pallas kernels, local(): pl.pallas_call(body, out_shape=(jax.ShapeDtypeStruct((row_blocks, LANES),...  61 us
    pallas_call x1, Pallas kernels, hand_on(): pl.pallas_call(move, out_shape=tuple((jax.ShapeDtypeStruct(a.shape, a.dty...  1.7 us

profile of v4, /device:TPU:1, one launch (start us, length us, event | category | flops | bytes accessed | tf_op | source)
XLA Modules:
  0.0 63.3 jit_solution(4509330174145081877)
XLA Ops:
  0.6 61.0 %sinkhorn.1 = (f32[4,128]{1,0:T(4,128)}, f32[64,128]{1,0:T(8,128)}, f32[512,128]{1,0:T(8,128)}) custom-call(bf16[512,128]{1,0:T(8,128)(2,1)} %refs_0_.1, bf16[8192,128]{1,0:T(8,128)(2,1)} %refs_1_.1, f32[4,128]{1,0:T(4,128)} %bitcast.5, f32[64,128]{1,0:T(8,128)} %bitcast.4), custom_call_target="tpu_custom_call" | custom-call | tf_op jit(solution)/shard_map/sinkhorn/pallas_call | solution.py:562
  61.6 1.7 %hand_on.1 = (f32[4,128]{1,0:T(4,128)}, f32[64,128]{1,0:T(8,128)}, f32[512,128]{1,0:T(8,128)}) custom-call(f32[4,128]{1,0:T(4,128)} %get-tuple-element.9.f, f32[64,128]{1,0:T(8,128)} %get-tuple-element.10.g, f32[512,128]{1,0:T(8,128)} %get-tuple-element.11.grad), custom_call_target="tpu_custom_call" | custom-call | tf_op jit(solution)/shard_map/hand_on/pallas_call | solution.py:537

commit v5 on v4

--- a/solution.py
+++ b/solution.py
@@ -21,7 +21,7 @@
 TILE2 = 4096
 WIDE = 16
 GROUPS3 = 16
-GROUPS4 = 4
+GROUPS4 = 8
 TILE5 = 2048
 ROWS5 = 128
 PARTS = 4
@@ -446,37 +446,43 @@
         arrived(CHIP4 + j, ag4.at[pl.ds(0, chips - 1), mine])
         col4[at, :] = rm[at, :] / (ref_total * jnp.sum(ag4[:, mine, :], axis=0))
     send(BACK4, {"row": partner}, col4.at[own_groups], col4.at[own_groups])
-    arrived(BACK4, col4.at[other_groups])
 
     n5 = TILE5 // LANES
     share = ROWS5 // ncol
 
-    def pass5(b, carry):
+    def pass5(b, first):
         base = pl.multiple_of(b * ROWS5, ROWS5)
         whole = pl.ds(base, ROWS5)
-        powers, u, masses = R.at[whole], lanes_u.at[whole], acc_a.at[whole]
+        u, masses = lanes_u.at[whole], acc_a.at[whole]
         chunks_here = ROWS5 // CHUNK
-        weights = W.at[pl.ds(pl.multiple_of(b * (chunks_here * SUB), SUB), chunks_here * SUB)]
+        weight_rows = pl.ds(pl.multiple_of(b * (chunks_here * SUB), SUB), chunks_here * SUB)
         pulled = jnp.zeros((ROWS5, width), f32)
-        for t in range(cols // TILE5):
+        in_half = half_groups // n5
+        for t in range(2 * in_half):
+            if first and t == in_half:
+                arrived(BACK4, col4.at[other_groups])
+            g0 = (own if t < in_half else other) * SUB + (t % in_half) * n5
+            here = pl.ds(pl.multiple_of(g0 * LANES, TILE5), TILE5)
+            powers, weights = R.at[whole, here], W.at[weight_rows, here]
+            ratios = col4.at[pl.ds(pl.multiple_of(g0, SUB), n5)]
             low = [[] for _ in range(n5)]
             for q in range(ROWS5 // CHUNK):
                 hq = slice(q * SUB, (q + 1) * SUB)
-                w = [weights[hq, (t * n5 + k) * LANES:(t * n5 + k + 1) * LANES] * col4[t * n5 + k:t * n5 + k + 1, :]
+                w = [weights[hq, k * LANES:(k + 1) * LANES] * ratios[k:k + 1, :]
                      for k in range(n5)]
                 for i in range(q * CHUNK, (q + 1) * CHUNK, SUB):
                     at = slice(i, i + SUB)
                     a = u[at, :]
                     mass = masses[at, :]
                     for k in range(n5):
-                        p = (powers[at, (t * n5 + k) * LANES:(t * n5 + k + 1) * LANES] * w[k]) * a
+                        p = (powers[at, k * LANES:(k + 1) * LANES] * w[k]) * a
                         mass = mass + p
                         low[k].append(p)
                     masses[at, :] = mass
             plan_low = jnp.concatenate(
                 [jnp.concatenate(v, axis=0).astype(jnp.bfloat16) for v in low], axis=1
             )
-            pulled = pulled + jnp.dot(plan_low, y[t * TILE5:(t + 1) * TILE5, :], preferred_element_type=f32)
+            pulled = pulled + jnp.dot(plan_low, y[here, :], preferred_element_type=f32)
         mass_row = jnp.sum(masses[...], axis=1, keepdims=True)
         part[whole, :] = mass_row * x[whole, :].astype(f32) - pulled
         to_cols(
@@ -485,9 +491,13 @@
             pr5.at[b, c],
         )
         pr5[b, c] = part[pl.ds(pl.multiple_of(base + c * share, share), share), :]
-        return carry
-
-    lax.fori_loop(0, rows // ROWS5, pass5, 0)
+
+    def pass5_later(b, carry):
+        pass5(b, False)
+        return carry
+
+    pass5(0, True)
+    lax.fori_loop(1, rows // ROWS5, pass5_later, 0)
 
     for j in range(tiles):
         at = slice(j * SUB, (j + 1) * SUB)

time: 63.5 us -> 63 us (level)
  no operation moved by 1% of the time
where the time goes in v5:
time: 63 us; the launch traced here: 62.8 us
  Pallas kernels  62.2 us (99%)
  between operations  0.64 us (1%)
    pallas_call x1, Pallas kernels, local(): pl.pallas_call(body, out_shape=(jax.ShapeDtypeStruct((row_blocks, LANES),...  60.5 us
    pallas_call x1, Pallas kernels, hand_on(): pl.pallas_call(move, out_shape=tuple((jax.ShapeDtypeStruct(a.shape, a.dty...  1.7 us

profile of v5, /device:TPU:1, one launch (start us, length us, event | category | flops | bytes accessed | tf_op | source)
XLA Modules:
  0.0 62.8 jit_solution(12958382170182066831)
XLA Ops:
  0.6 60.5 %sinkhorn.1 = (f32[4,128]{1,0:T(4,128)}, f32[64,128]{1,0:T(8,128)}, f32[512,128]{1,0:T(8,128)}) custom-call(bf16[512,128]{1,0:T(8,128)(2,1)} %refs_0_.1, bf16[8192,128]{1,0:T(8,128)(2,1)} %refs_1_.1, f32[4,128]{1,0:T(4,128)} %bitcast.5, f32[64,128]{1,0:T(8,128)} %bitcast.4), custom_call_target="tpu_custom_call" | custom-call | tf_op jit(solution)/shard_map/sinkhorn/pallas_call | solution.py:572
  61.1 1.7 %hand_on.1 = (f32[4,128]{1,0:T(4,128)}, f32[64,128]{1,0:T(8,128)}, f32[512,128]{1,0:T(8,128)}) custom-call(f32[4,128]{1,0:T(4,128)} %get-tuple-element.9.f, f32[64,128]{1,0:T(8,128)} %get-tuple-element.10.g, f32[512,128]{1,0:T(8,128)} %get-tuple-element.11.grad), custom_call_target="tpu_custom_call" | custom-call | tf_op jit(solution)/shard_map/hand_on/pallas_call | solution.py:547
